TPU v7x, 256 devices: a whole 4x4x8 slice. The times are simulated.
256 devices in a mesh: kx: 8 (over x_lo, y), kz: 32 (over z, x_hi, core).
Axes of the slice: x: 4 (x_hi: 2, x_lo: 2; x = x_hi * 2 + x_lo), y: 4, z: 8, core: 2. Of those that a mesh axis runs over, the one named last changes fastest.
Arguments:
- forcing: float32 [1536, 4, 128, 256], P(('kx', 'kz')), may hold values from -20 to 20
- kx_wave: int32 [128], P('kx'), may hold values from 0 to 64
- kz_wave: int32 [256], P('kz'), may hold values from -32 to 32
Outputs:
- fields: float32 [1536, 4, 128, 256], P(('kx', 'kz'))
All inputs are finite; a program needn't handle non-finite values.
Results may differ from a plain program's by a relative error of at most 0.00007.
Values sent between devices are 32-bit elements; how exact they have to be, the bound alone decides.
No kernel may reach another device: no remote copies, remote signals or barrier semaphores. Data moves between devices by JAX's collectives and lax.ppermute only.
A program may use at most 192 MiB of HBM per device.

v0:
```python
import functools
import math

import jax
import jax.numpy as jnp
from jax import lax
from jax.experimental import pallas as pl
from jax.experimental.pallas import tpu as pltpu
from jax.sharding import PartitionSpec as P

NY = 1536
N = NY + 1
H2 = (2.0 / N) ** 2
SHIFT = 4000.0
KAPPA = SHIFT * H2
ALPHA_X = 0.25
BETA_Z = 2.0 / 3.0
PTS = 6
BLK = 12
GRP = 16
F32 = jnp.float32


def chain(eps, n):
    p = [None, jnp.ones_like(eps)]
    diff = 1.0 + eps
    for _ in range(2, n + 1):
        p.append(p[-1] + diff)
        diff = diff + eps * p[-1]
    return p


def angle(eps):
    x2 = 0.25 * eps
    series = 1.0 + x2 * (-1.0 / 6.0 + x2 * (3.0 / 40.0 + x2 * (-15.0 / 336.0 + x2 * (105.0 / 3456.0))))
    return jnp.sqrt(eps) * series


def moments_kernel(s_ref, w_ref, x_ref, r_ref, up_ref, mid_ref, q_ref, qo_ref):
    core = s_ref[0]
    turn = s_ref[3]
    step = pl.program_id(0)
    lane = lax.broadcasted_iota(jnp.int32, (8, 128), 1) // 8
    sub = lax.broadcasted_iota(jnp.int32, (8, 128), 0)

    def kz_row(half):
        acc = [jnp.zeros((8, 128), F32), jnp.zeros((8, 128), F32)]
        for j in range(32):
            place = lax.rem(j // 4 + turn, 8) + 8 * (j % 4) - GRP * half
            acc[j % 2] = acc[j % 2] + jnp.where(lane == place, w_ref[j], 0.0)
        row = acc[0][4:5, :] + acc[1][0:1, :]
        return jnp.broadcast_to(row, (8, 128))

    kz_own = (BETA_Z * kz_row(core)) ** 2
    kz_oth = (BETA_Z * kz_row(1 - core)) ** 2
    tiles = up_ref.shape[0]

    def tile(first, second):
        for i in range(tiles):
            at = 2 * (step * tiles + i)
            kx = (ALPHA_X * jnp.where(sub < 4, w_ref[at], w_ref[at + 1])) ** 2
            rows = pl.ds(8 * i, 8)
            q = kx + kz_own
            q_ref[rows, :] = q
            qo_ref[rows, :] = kx + kz_oth
            ps = chain(H2 * (q + SHIFT), BLK)
            pq = chain(H2 * q, BLK)
            for c in range(4):
                f = [first[m, c, rows, :] for m in range(PTS)] + [second[m, c, rows, :] for m in range(PTS)]
                own = ps[BLK] * f[0]
                nxt = ps[1] * f[1]
                mid = ps[1] * f[1]
                for m in range(1, BLK):
                    own = own + ps[BLK - m] * f[m]
                for m in range(2, BLK):
                    nxt = nxt + ps[m] * f[m]
                    mid = mid + ps[min(m, BLK - m)] * f[m]
                up_ref[i, c] = KAPPA * own
                up_ref[i, 4 + c] = KAPPA * nxt
                mid_ref[i, c] = KAPPA * mid
                if c < 2:
                    own = pq[BLK] * f[0]
                    nxt = pq[1] * f[1]
                    for m in range(1, BLK):
                        own = own + pq[BLK - m] * f[m]
                    for m in range(2, BLK):
                        nxt = nxt + pq[m] * f[m]
                    up_ref[i, 8 + c] = KAPPA * own
                    up_ref[i, 10 + c] = KAPPA * nxt

    @pl.when(core == 0)
    def _():
        tile(x_ref, r_ref)

    @pl.when(core != 0)
    def _():
        tile(r_ref, x_ref)


def sources(m_ref, own, nxt):
    return (
        [m_ref[0, own]]
        + [m_ref[d, own] + m_ref[d - 1, nxt] for d in range(1, GRP)]
        + [m_ref[GRP - 1, nxt]]
    )


def group_kernel(s_ref, m_ref, q_ref, o_ref):
    group = s_ref[1]
    q = q_ref[...]
    rho = jnp.exp(-BLK * angle(H2 * (q + SHIFT)))
    res = [None] * 12
    for c in range(4):
        t = sources(m_ref, c, 4 + c)
        right = t[0]
        for d in range(1, GRP + 1):
            right = rho * right + t[d]
        left = t[GRP]
        for d in range(GRP - 1, -1, -1):
            left = rho * left + t[d]
        res[c] = right
        res[4 + c] = left
    tq = angle(H2 * q)
    end = jnp.exp(-N * tq)
    inv = 1.0 / jnp.where(q > 0.0, 1.0 - end * end, 1.0)
    sq = [sources(m_ref, 8 + c, 10 + c) for c in range(2)]
    for c in range(2):
        res[8 + c] = jnp.zeros_like(q)
        res[10 + c] = jnp.zeros_like(q)
    for d in range(GRP + 1):
        place = (BLK * (GRP * group + d) + 1).astype(F32)
        fall = jnp.exp(-place * tq)
        rise = (jnp.exp((place - N) * tq) - end * fall) * inv
        rise = jnp.where(q > 0.0, rise, place * (1.0 / N))
        fall = fall - end * rise
        for c in range(2):
            res[8 + c] = res[8 + c] + fall * sq[c][d]
            res[10 + c] = res[10 + c] + rise * sq[c][d]
    for k in range(o_ref.shape[0]):
        for n in range(12):
            o_ref[k, n] = res[n]


def solve_kernel(s_ref, m_ref, g_ref, q_ref, o_ref):
    group = s_ref[1]
    groups = g_ref.shape[0]
    q = q_ref[...]
    es = H2 * (q + SHIFT)
    eq = H2 * q
    ts = angle(es)
    tq = angle(eq)
    rho = jnp.exp(-BLK * ts)
    rho_g = jnp.exp(-(BLK * GRP) * ts)
    sinh_s = jnp.sqrt(es * (1.0 + 0.25 * es))
    sinh_q = jnp.sqrt(eq * (1.0 + 0.25 * eq))
    scale = 0.5 / (sinh_s * chain(es, BLK)[BLK])
    end_s = jnp.exp(-N * ts)
    inv_s = 1.0 / (1.0 - end_s * end_s)
    end_q = jnp.exp(-N * tq)
    positive = q > 0.0
    inv_q = 1.0 / jnp.where(positive, 1.0 - end_q * end_q, 1.0)
    coth_s = sinh_s * (1.0 + end_s * end_s) * inv_s
    csch_s = 2.0 * sinh_s * end_s * inv_s
    coth_q = jnp.where(positive, sinh_q * (1.0 + end_q * end_q) * inv_q, 1.0 / N)
    csch_q = jnp.where(positive, 2.0 * sinh_q * end_q * inv_q, 1.0 / N)
    m_same = (2.0 - es) * coth_s - (2.0 - eq) * coth_q + 0.5 * (es * es - eq * eq)
    m_cross = (2.0 - eq) * csch_q - (2.0 - es) * csch_s
    inv_det = 1.0 / (m_same * m_same - m_cross * m_cross)
    inv_pq = 1.0 / chain(eq, BLK)[BLK]
    gf = group.astype(F32)
    near = jnp.exp(-(gf * (BLK * GRP) + 1.0) * ts)
    far = jnp.exp(-(NY - BLK * GRP - gf * (BLK * GRP)) * ts)
    first = jnp.exp(-ts)
    for c in range(4):
        at_hi = g_ref[0, c]
        from_lo = jnp.zeros_like(q)
        for k in range(groups):
            if k:
                at_hi = rho_g * at_hi + g_ref[k, c]
            from_lo = jnp.where(k < group, rho_g * from_lo + g_ref[k, c], from_lo)
        at_lo = g_ref[groups - 1, 4 + c]
        from_hi = jnp.zeros_like(q)
        for k in range(groups - 1, -1, -1):
            if k < groups - 1:
                at_lo = rho_g * at_lo + g_ref[k, 4 + c]
            from_hi = jnp.where(k > group, rho_g * from_hi + g_ref[k, 4 + c], from_hi)
        x_lo = scale * first * at_lo
        x_hi = scale * at_hi
        if c < 2:
            y_lo = g_ref[0, 8 + c]
            y_hi = g_ref[0, 10 + c]
            for k in range(1, groups):
                y_lo = y_lo + g_ref[k, 8 + c]
                y_hi = y_hi + g_ref[k, 10 + c]
            alpha = (end_s * x_hi - x_lo) * inv_s
            beta = (end_s * x_lo - x_hi) * inv_s
            phi_lo = 2.0 * sinh_s * (x_lo + end_s * beta)
            phi_hi = 2.0 * sinh_s * (x_hi + end_s * alpha)
            w_lo = (2.0 - es) * phi_lo - (2.0 - eq) * (y_lo * inv_pq)
            w_hi = (2.0 - es) * phi_hi - (2.0 - eq) * (y_hi * inv_pq)
            wall_lo = (m_same * w_lo - m_cross * w_hi) * inv_det - x_lo
            wall_hi = (m_same * w_hi - m_cross * w_lo) * inv_det - x_hi
        else:
            wall_lo = -x_lo
            wall_hi = -x_hi
        alpha = (wall_lo - end_s * wall_hi) * inv_s
        beta = (wall_hi - end_s * wall_lo) * inv_s
        t = [scale * v for v in sources(m_ref, c, 4 + c)]
        back = scale * from_hi + beta * far
        falls = [None] * (GRP + 1)
        falls[GRP] = back
        for d in range(GRP - 1, -1, -1):
            back = rho * (back + t[d + 1])
            falls[d] = back
        ahead = scale * from_lo + alpha * near + t[0]
        for d in range(GRP + 1):
            if d:
                ahead = rho * ahead + t[d]
            value = ahead + falls[d]
            if d < GRP:
                o_ref[d, c] = value
            if d:
                o_ref[d - 1, 4 + c] = value


def middle_kernel(s_ref, b_ref, mid_ref, q_ref, own_ref, send_ref):
    core = s_ref[0]

    def tile(lower, upper):
        for i in range(b_ref.shape[0]):
            ps = chain(H2 * (q_ref[pl.ds(8 * i, 8), :] + SHIFT), BLK)
            ratio = ps[PTS] / ps[BLK]
            for c in range(4):
                a = b_ref[i, c]
                b = b_ref[i, 4 + c]
                x = ratio * (a + b + mid_ref[i, c])
                lower[i, c] = a
                lower[i, 4 + c] = x
                upper[i, c] = x
                upper[i, 4 + c] = b

    @pl.when(core == 0)
    def _():
        tile(own_ref, send_ref)

    @pl.when(core != 0)
    def _():
        tile(send_ref, own_ref)


def points_kernel(s_ref, x_ref, own_ref, r_ref, q_ref, qo_ref, o_ref):
    core = s_ref[0]

    def tile(half, ends, waves):
        lanes = pl.ds(128 * half, 128)
        for i in range(ends.shape[0]):
            rows = pl.ds(8 * i, 8)
            ps = chain(H2 * (waves[rows, :] + SHIFT), PTS)
            ratio = [None] + [ps[m] / ps[m + 1] for m in range(1, PTS)]
            for c in range(4):
                a = ends[i, c]
                y = [None, KAPPA * x_ref[1, c, rows, lanes] + a]
                for m in range(2, PTS):
                    y.append(KAPPA * x_ref[m, c, rows, lanes] + ratio[m - 1] * y[-1])
                o_ref[0, c, rows, lanes] = a
                value = ends[i, 4 + c]
                for m in range(PTS - 1, 0, -1):
                    value = ratio[m] * (y[m] + value)
                    o_ref[m, c, rows, lanes] = value

    @pl.when(core == 0)
    def _():
        tile(0, own_ref, q_ref)
        tile(1, r_ref, qo_ref)

    @pl.when(core != 0)
    def _():
        tile(0, r_ref, qo_ref)
        tile(1, own_ref, q_ref)


def on_device(forcing, kx_wave, kz_wave):
    ix = lax.axis_index("kx")
    iz = lax.axis_index("kz")
    core = lax.rem(iz, 2)
    chip = iz // 2
    turn = lax.rem(iz - ix + 32, 8)
    place = jnp.stack([core, ix, chip, turn]).astype(jnp.int32)
    both = ("kx", "kz")
    wave_groups = [
        [k * 32 + (k + t) % 8 + 8 * part for k in range(8) for part in range(4)] for t in range(8)
    ]
    core_groups = [[2 * k + c for k in range(GRP)] for c in range(2)]
    pairs = [(i, i ^ 1) for i in range(32)]

    other = lax.dynamic_slice_in_dim(forcing, 128 * (1 - core), 128, axis=3)
    swapped = lax.ppermute(other, "kz", pairs)

    part = iz // 8
    kx8 = lax.dynamic_slice_in_dim(kx_wave, 8 * (part // 2), 8).astype(F32)
    sub = lax.broadcasted_iota(jnp.int32, (8, 128), 0)
    payload = jnp.where(
        sub // 4 == lax.rem(part, 2),
        jnp.broadcast_to(kx8[:, None], (8, 128)),
        jnp.broadcast_to(jnp.tile(kz_wave.astype(F32), 16)[None, :], (8, 128)),
    )
    waves = lax.all_to_all(
        jnp.broadcast_to(payload[None], (32, 8, 128)), both, 0, 0, tiled=True, axis_index_groups=wave_groups
    )

    steps = 4
    tiles = GRP // steps
    rows = 8 * tiles
    tiled = lambda n: pl.BlockSpec((tiles, n, 8, 128), lambda i, s: (i, 0, 0, 0))
    flat = pl.BlockSpec((rows, 128), lambda i, s: (i, 0))
    up, mid, q_own, q_oth = pl.pallas_call(
        moments_kernel,
        grid_spec=pltpu.PrefetchScalarGridSpec(
            num_scalar_prefetch=1,
            grid=(steps,),
            in_specs=[
                pl.BlockSpec((32, 8, 128), lambda i, s: (0, 0, 0)),
                pl.BlockSpec((PTS, 4, rows, 128), lambda i, s: (0, 0, i, s[0])),
                pl.BlockSpec((PTS, 4, rows, 128), lambda i, s: (0, 0, i, 0)),
            ],
            out_specs=[tiled(12), tiled(4), flat, flat],
        ),
        out_shape=[
            jax.ShapeDtypeStruct((GRP, 12, 8, 128), F32),
            jax.ShapeDtypeStruct((GRP, 4, 8, 128), F32),
            jax.ShapeDtypeStruct((128, 128), F32),
            jax.ShapeDtypeStruct((128, 128), F32),
        ],
    )(place, waves, forcing, swapped)

    blocks = lax.all_to_all(up, "kz", 0, 0, tiled=True, axis_index_groups=core_groups)

    whole = lambda *shape: pl.BlockSpec(shape, lambda i, s: (0,) * len(shape))
    my_q = pl.BlockSpec((8, 128), lambda i, s: (s[2], 0))
    message = pl.pallas_call(
        group_kernel,
        grid_spec=pltpu.PrefetchScalarGridSpec(
            num_scalar_prefetch=1,
            grid=(1,),
            in_specs=[whole(GRP, 12, 8, 128), my_q],
            out_specs=whole(8, 12, 8, 128),
        ),
        out_shape=jax.ShapeDtypeStruct((8, 12, 8, 128), F32),
    )(place, blocks, q_own)

    messages = lax.all_to_all(message, "kx", 0, 0, tiled=True)

    ends = pl.pallas_call(
        solve_kernel,
        grid_spec=pltpu.PrefetchScalarGridSpec(
            num_scalar_prefetch=1,
            grid=(1,),
            in_specs=[whole(GRP, 12, 8, 128), whole(8, 12, 8, 128), my_q],
            out_specs=whole(GRP, 8, 8, 128),
        ),
        out_shape=jax.ShapeDtypeStruct((GRP, 8, 8, 128), F32),
    )(place, blocks, messages, q_own)

    ends = lax.all_to_all(ends, "kz", 0, 0, tiled=True, axis_index_groups=core_groups)

    own, send = pl.pallas_call(
        middle_kernel,
        grid_spec=pltpu.PrefetchScalarGridSpec(
            num_scalar_prefetch=1,
            grid=(steps,),
            in_specs=[tiled(8), tiled(4), flat],
            out_specs=[tiled(8), tiled(8)],
        ),
        out_shape=[jax.ShapeDtypeStruct((GRP, 8, 8, 128), F32)] * 2,
    )(place, ends, mid, q_own)

    received = lax.ppermute(send, "kz", pairs)

    return pl.pallas_call(
        points_kernel,
        grid_spec=pltpu.PrefetchScalarGridSpec(
            num_scalar_prefetch=1,
            grid=(steps,),
            in_specs=[
                pl.BlockSpec((PTS, 4, rows, 256), lambda i, s: (0, 0, i, 0)),
                tiled(8),
                tiled(8),
                flat,
                flat,
            ],
            out_specs=pl.BlockSpec((PTS, 4, rows, 256), lambda i, s: (0, 0, i, 0)),
        ),
        out_shape=jax.ShapeDtypeStruct(forcing.shape, F32),
    )(place, forcing, own, received, q_own, q_oth)


def solution(mesh):
    placed = (P(("kx", "kz"), None, None, None), P("kx"), P("kz"))
    return jax.shard_map(
        on_device,
        mesh=mesh,
        in_specs=placed,
        out_specs=P(("kx", "kz"), None, None, None),
        check_vma=False,
    )
```

profile of v0, /device:TPU:1, one launch (start us, length us, event | category | flops | bytes accessed | tf_op | source)
XLA Modules:
  0.0 116.9 jit_solution(10015997536259778551)
XLA Ops:
  0.0 0.0 copy-start.4
  0.0 0.0 copy-start.3
  0.0 1.5 %constant_dynamic-slice_fusion = f32[6,4,128,128]{3,2,1,0:T(8,128)S(1)} fusion(f32[6,4,128,256]{3,2,1,0:T(8,128)} %x_ref.3, s32[]{:T(128)S(6)} %select_n.40), kind=kLoop, calls=%fused_computation.9 | loop fusion | bytes 3145732 | tf_op jit(solution)/shard_map/dynamic_slice | solution.py:296
  1.5 3.3 %collective-permute-start = (f32[6,4,128,128]{3,2,1,0:T(8,128)S(1)}, f32[6,4,128,128]{3,2,1,0:T(8,128)S(1)}, u32[]{:S(2)}, u32[]{:S(2)}) collective-permute-start(f32[6,4,128,128]{3,2,1,0:T(8,128)S(1)} %constant_dynamic-slice_fusion), channel_id=1, source_target_pairs={{0,1},{1,0},{2,3},{3,2},{4,5},{5,4},{6,7},{7,6},{8,9},{9,8},{10,11... | collective-permute-start | bytes 4718600 | tf_op jit(solution)/shard_map/ppermute | solution.py:297
  4.9 0.0 copy-done.4
  4.9 0.1 broadcast_in_dim.9
  5.0 0.0 copy-done.3
  5.0 0.1 iota_shift-right-logical_fusion
  5.1 0.1 fusion
  5.2 0.7 broadcast_in_dim.22
  5.8 11.9 %all-to-all-start = ((f32[32,8,128]{2,1,0:T(8,128)}), f32[32,8,128]{2,1,0:T(8,128)S(1)}, u32[]{:S(2)}, u32[]{:S(2)}) async-start(f32[32,8,128]{2,1,0:T(8,128)} %broadcast_in_dim.22), calls=%async_computation | async-start | bytes 262144 | tf_op jit(solution)/shard_map/all_to_all | solution.py:307
  17.8 0.6 pad_add_fusion.s_ref
  18.4 10.6 %all-to-all-done.w_ref = f32[32,8,128]{2,1,0:T(8,128)S(1)} async-done(((f32[32,8,128]{2,1,0:T(8,128)}), f32[32,8,128]{2,1,0:T(8,128)S(1)}, u32[]{:S(2)}, u32[]{:S(2)}) %all-to-all-start) | async-done | bytes 131104 | tf_op jit(solution)/shard_map/all_to_all | solution.py:307
  29.1 0.0 copy-start.2
  29.1 0.0 collective-permute-done.r_ref
  29.1 0.6 copy-done.2
  29.7 0.0 copy-start
  29.7 1.1 copy-done
  30.9 5.0 %shard_map.37 = (f32[16,12,8,128]{3,2,1,0:T(8,128)}, f32[16,4,8,128]{3,2,1,0:T(8,128)}, f32[128,128]{1,0:T(8,128)}, f32[128,128]{1,0:T(8,128)}) custom-call(s32[4]{0:T(128)} %pad_add_fusion.s_ref, f32[32,8,128]{2,1,0:T(8,128)} %copy-done.2, f32[6,4,128,256]{3,2,1,0:T(8,128)} %x_ref.3, f32[6,4,128,128]{3,2,1,0:T(8,128)} %copy-done), custom_call_target="tpu_custom_call" | custom-call | tf_op jit(solution)/shard_map/pallas_call | solution.py:316
  35.9 26.7 %all_to_all.20.m_ref = f32[16,12,8,128]{3,2,1,0:T(8,128)} all-to-all(f32[16,12,8,128]{3,2,1,0:T(8,128)} %get-tuple-element.11), channel_id=1, replica_groups={{0,2,4,6,8,10,12,14,16,18,20,22,24,26,28,30},{1,3,5,7,9,11,13,15,17,19,..., dimensions={0} | all-to-all | bytes 1572864 | tf_op jit(solution)/shard_map/all_to_all | solution.py:336
  62.6 2.7 %shard_map.38 = f32[8,12,8,128]{3,2,1,0:T(8,128)} custom-call(s32[4]{0:T(128)} %pad_add_fusion.s_ref, f32[16,12,8,128]{3,2,1,0:T(8,128)} %all_to_all.20.m_ref, f32[128,128]{1,0:T(8,128)} %get-tuple-element.12.q_ref), custom_call_target="tpu_custom_call" | custom-call | tf_op jit(solution)/shard_map/pallas_call | solution.py:340
  65.3 12.8 %all_to_all.21.g_ref = f32[8,12,8,128]{3,2,1,0:T(8,128)} all-to-all(f32[8,12,8,128]{3,2,1,0:T(8,128)} %shard_map.38), channel_id=1, replica_groups=mesh['kx'=8,'kz'=32] {'kx'}, dimensions={0} | all-to-all | bytes 786432 | tf_op jit(solution)/shard_map/all_to_all | solution.py:351
  78.1 2.9 %shard_map.39 = f32[16,8,8,128]{3,2,1,0:T(8,128)} custom-call(s32[4]{0:T(128)} %pad_add_fusion.s_ref, f32[16,12,8,128]{3,2,1,0:T(8,128)} %all_to_all.20.m_ref, f32[8,12,8,128]{3,2,1,0:T(8,128)} %all_to_all.21.g_ref, f32[128,128]{1,0:T(8,128)} %get-tuple-element.12.q_ref), custom_call_target="tpu_custom_call" | custom-call | tf_op jit(solution)/shard_map/pallas_call | solution.py:353
  81.0 19.3 %all_to_all.22.b_ref = f32[16,8,8,128]{3,2,1,0:T(8,128)} all-to-all(f32[16,8,8,128]{3,2,1,0:T(8,128)} %shard_map.39), channel_id=1, replica_groups={{0,2,4,6,8,10,12,14,16,18,20,22,24,26,28,30},{1,3,5,7,9,11,13,15,17,19,..., dimensions={0} | all-to-all | bytes 1048576 | tf_op jit(solution)/shard_map/all_to_all | solution.py:364
  100.3 4.1 %shard_map.40 = (f32[16,8,8,128]{3,2,1,0:T(8,128)}, f32[16,8,8,128]{3,2,1,0:T(8,128)}) custom-call(s32[4]{0:T(128)} %pad_add_fusion.s_ref, f32[16,8,8,128]{3,2,1,0:T(8,128)} %all_to_all.22.b_ref, f32[16,4,8,128]{3,2,1,0:T(8,128)} %get-tuple-element.13.mid_ref, f32[128,128]{1,0:T(8,128)} %get-tuple-element.12.q_ref), custom_call_target="tpu_custom_call" | custom-call | tf_op jit(solution)/shard_map/pallas_call | solution.py:366
  104.4 4.7 %collective-permute-start.1 = (f32[16,8,8,128]{3,2,1,0:T(8,128)}, f32[16,8,8,128]{3,2,1,0:T(8,128)S(1)}, u32[]{:S(2)}, u32[]{:S(2)}) collective-permute-start(f32[16,8,8,128]{3,2,1,0:T(8,128)} %get-tuple-element.15), channel_id=1, source_target_pairs={{0,1},{1,0},{2,3},{3,2},{4,5},{5,4},{6,7},{7,6},{8,9},{9,8},{10,11... | collective-permute-start | bytes 1572872 | tf_op jit(solution)/shard_map/ppermute | solution.py:377
  109.1 1.7 %collective-permute-done.1.r_ref = f32[16,8,8,128]{3,2,1,0:T(8,128)S(1)} collective-permute-done((f32[16,8,8,128]{3,2,1,0:T(8,128)}, f32[16,8,8,128]{3,2,1,0:T(8,128)S(1)}, u32[]{:S(2)}, u32[]{:S(2)}) %collective-permute-start.1) | collective-permute-done | bytes 524320 | tf_op jit(solution)/shard_map/ppermute | solution.py:377
  110.9 0.0 copy-start.1
  110.9 0.8 copy-done.1
  111.7 5.3 %shard_map.41 = f32[6,4,128,256]{3,2,1,0:T(8,128)} custom-call(s32[4]{0:T(128)} %pad_add_fusion.s_ref, f32[6,4,128,256]{3,2,1,0:T(8,128)} %x_ref.3, f32[16,8,8,128]{3,2,1,0:T(8,128)} %get-tuple-element.14.own_ref, f32[16,8,8,128]{3,2,1,0:T(8,128)} %copy-done.1, f32[128,128]{1,0:T(8,128)} %get-tuple-element.12.q_ref, f32[128,128]{1,0:T(8,128)} %get-tuple-element.16.qo_ref), custom_call_target="tpu_custom_call" | custom-call | tf_op jit(solution)/shard_map/pallas_call | solution.py:379
  (4 shorter events, 0.0 us)
Async XLA Ops:
  0.0 4.9 %copy-start.4 = (s32[8]{0:T(128)S(1)}, s32[8]{0:T(128)}, u32[]{:S(2)}) copy-start(s32[8]{0:T(128)} %param.5) | copy-start | bytes 100
  0.0 5.0 %copy-start.3 = (s32[16]{0:T(128)S(1)}, s32[16]{0:T(128)}, u32[]{:S(2)}) copy-start(s32[16]{0:T(128)} %param.4) | copy-start | bytes 196
  1.5 27.5 %collective-permute-start = (f32[6,4,128,128]{3,2,1,0:T(8,128)S(1)}, f32[6,4,128,128]{3,2,1,0:T(8,128)S(1)}, u32[]{:S(2)}, u32[]{:S(2)}) collective-permute-start(f32[6,4,128,128]{3,2,1,0:T(8,128)S(1)} %constant_dynamic-slice_fusion), channel_id=1, source_target_pairs={{0,1},{1,0},{2,3},{3,2},{4,5},{5,4},{6,7},{7,6},{8,9},{9,8},{10,11... | collective-permute-start | bytes 4718600 | tf_op jit(solution)/shard_map/ppermute | solution.py:297
  5.8 23.2 %all-to-all-start = ((f32[32,8,128]{2,1,0:T(8,128)}), f32[32,8,128]{2,1,0:T(8,128)S(1)}, u32[]{:S(2)}, u32[]{:S(2)}) async-start(f32[32,8,128]{2,1,0:T(8,128)} %broadcast_in_dim.22), calls=%async_computation | async-start | bytes 262144 | tf_op jit(solution)/shard_map/all_to_all | solution.py:307
  29.1 0.7 copy-start.2
  29.7 1.1 copy-start
  104.4 6.5 %collective-permute-start.1 = (f32[16,8,8,128]{3,2,1,0:T(8,128)}, f32[16,8,8,128]{3,2,1,0:T(8,128)S(1)}, u32[]{:S(2)}, u32[]{:S(2)}) collective-permute-start(f32[16,8,8,128]{3,2,1,0:T(8,128)} %get-tuple-element.15), channel_id=1, source_target_pairs={{0,1},{1,0},{2,3},{3,2},{4,5},{5,4},{6,7},{7,6},{8,9},{9,8},{10,11... | collective-permute-start | bytes 1572872 | tf_op jit(solution)/shard_map/ppermute | solution.py:377
  110.9 0.8 copy-start.1
where the time goes:
time: 118 us; the launch traced here: 117 us
  blocking collectives  58.8 us (50%)
  starting transfers between devices  20 us (17%)
  Pallas kernels  19.9 us (17%)
  waiting for transfers between devices  12.4 us (11%)
  local copies, waits for them, and re-layouts  4.88 us (4%)
    all_to_all x1, blocking collectives, on_device(): lax.all_to_all(up, 'kz', 0, 0, tiled=True, axis_index_groups=core_groups)  26.7 us
    all_to_all x1, blocking collectives, on_device(): lax.all_to_all(ends, 'kz', 0, 0, tiled=True, axis_index_groups=core_groups)  19.3 us
    all_to_all x1, blocking collectives, on_device(): messages = lax.all_to_all(message, 'kx', 0, 0, tiled=True)  12.8 us
    all_to_all x1, starting transfers between devices, on_device(): lax.all_to_all(jnp.broadcast_to(payload[None], (32, 8, 128)), both, 0, 0,...  11.9 us
    all_to_all x1, waiting for transfers between devices, on_device(): lax.all_to_all(jnp.broadcast_to(payload[None], (32, 8, 128)), both, 0, 0,...  10.6 us
    pallas_call x1, Pallas kernels, on_device(): pl.pallas_call(points_kernel, grid_spec=pltpu.PrefetchScalarGridSpec(num_...  5.27 us
    pallas_call x1, Pallas kernels, on_device(): pl.pallas_call(moments_kernel, grid_spec=pltpu.PrefetchScalarGridSpec(num...  5.01 us
    ppermute x1, starting transfers between devices, on_device(): received = lax.ppermute(send, 'kz', pairs)  4.72 us
  transfers between devices with their start and end apart: 3, of which 2 were waited for; matrix products, arithmetic and copies ran while one was open for 1% of the time, Pallas kernels for 0%

commit v1 on v0

--- a/solution.py
+++ b/solution.py
@@ -1,6 +1,3 @@
-import functools
-import math
-
 import jax
 import jax.numpy as jnp
 from jax import lax
@@ -39,7 +36,6 @@
 def moments_kernel(s_ref, w_ref, x_ref, r_ref, up_ref, mid_ref, q_ref, qo_ref):
     core = s_ref[0]
     turn = s_ref[3]
-    step = pl.program_id(0)
     lane = lax.broadcasted_iota(jnp.int32, (8, 128), 1) // 8
     sub = lax.broadcasted_iota(jnp.int32, (8, 128), 0)
 
@@ -49,24 +45,23 @@
             place = lax.rem(j // 4 + turn, 8) + 8 * (j % 4) - GRP * half
             acc[j % 2] = acc[j % 2] + jnp.where(lane == place, w_ref[j], 0.0)
         row = acc[0][4:5, :] + acc[1][0:1, :]
-        return jnp.broadcast_to(row, (8, 128))
-
-    kz_own = (BETA_Z * kz_row(core)) ** 2
-    kz_oth = (BETA_Z * kz_row(1 - core)) ** 2
-    tiles = up_ref.shape[0]
-
-    def tile(first, second):
-        for i in range(tiles):
-            at = 2 * (step * tiles + i)
-            kx = (ALPHA_X * jnp.where(sub < 4, w_ref[at], w_ref[at + 1])) ** 2
-            rows = pl.ds(8 * i, 8)
+        return (BETA_Z * jnp.broadcast_to(row, (8, 128))) ** 2
+
+    kz_own = kz_row(core)
+    kz_oth = kz_row(1 - core)
+
+    def tiles(first, second):
+        @pl.loop(0, GRP)
+        def _(i):
+            kx = (ALPHA_X * jnp.where(sub < 4, w_ref[2 * i], w_ref[2 * i + 1])) ** 2
+            rows = pl.ds(pl.multiple_of(8 * i, 8), 8)
             q = kx + kz_own
             q_ref[rows, :] = q
             qo_ref[rows, :] = kx + kz_oth
             ps = chain(H2 * (q + SHIFT), BLK)
             pq = chain(H2 * q, BLK)
             for c in range(4):
-                f = [first[m, c, rows, :] for m in range(PTS)] + [second[m, c, rows, :] for m in range(PTS)]
+                f = [first(m, c, rows) for m in range(PTS)] + [second(m, c, rows) for m in range(PTS)]
                 own = ps[BLK] * f[0]
                 nxt = ps[1] * f[1]
                 mid = ps[1] * f[1]
@@ -90,11 +85,11 @@
 
     @pl.when(core == 0)
     def _():
-        tile(x_ref, r_ref)
+        tiles(lambda m, c, rows: x_ref[m, c, rows, :128], lambda m, c, rows: r_ref[m, c, rows, :128])
 
     @pl.when(core != 0)
     def _():
-        tile(r_ref, x_ref)
+        tiles(lambda m, c, rows: r_ref[m, c, rows, 128:], lambda m, c, rows: x_ref[m, c, rows, 128:])
 
 
 def sources(m_ref, own, nxt):
@@ -107,7 +102,7 @@
 
 def group_kernel(s_ref, m_ref, q_ref, o_ref):
     group = s_ref[1]
-    q = q_ref[...]
+    q = q_ref[pl.ds(pl.multiple_of(8 * s_ref[2], 8), 8), :]
     rho = jnp.exp(-BLK * angle(H2 * (q + SHIFT)))
     res = [None] * 12
     for c in range(4):
@@ -144,7 +139,7 @@
 def solve_kernel(s_ref, m_ref, g_ref, q_ref, o_ref):
     group = s_ref[1]
     groups = g_ref.shape[0]
-    q = q_ref[...]
+    q = q_ref[pl.ds(pl.multiple_of(8 * s_ref[2], 8), 8), :]
     es = H2 * (q + SHIFT)
     eq = H2 * q
     ts = angle(es)
@@ -226,9 +221,10 @@
 def middle_kernel(s_ref, b_ref, mid_ref, q_ref, own_ref, send_ref):
     core = s_ref[0]
 
-    def tile(lower, upper):
-        for i in range(b_ref.shape[0]):
-            ps = chain(H2 * (q_ref[pl.ds(8 * i, 8), :] + SHIFT), BLK)
+    def tiles(lower, upper):
+        @pl.loop(0, GRP)
+        def _(i):
+            ps = chain(H2 * (q_ref[pl.ds(pl.multiple_of(8 * i, 8), 8), :] + SHIFT), BLK)
             ratio = ps[PTS] / ps[BLK]
             for c in range(4):
                 a = b_ref[i, c]
@@ -241,42 +237,69 @@
 
     @pl.when(core == 0)
     def _():
-        tile(own_ref, send_ref)
+        tiles(own_ref, send_ref)
 
     @pl.when(core != 0)
     def _():
-        tile(send_ref, own_ref)
-
-
-def points_kernel(s_ref, x_ref, own_ref, r_ref, q_ref, qo_ref, o_ref):
+        tiles(send_ref, own_ref)
+
+
+def points_kernel(s_ref, x_ref, own_ref, r_ref, q_ref, qo_ref, o_ref, buf, sems):
     core = s_ref[0]
-
-    def tile(half, ends, waves):
-        lanes = pl.ds(128 * half, 128)
-        for i in range(ends.shape[0]):
-            rows = pl.ds(8 * i, 8)
-            ps = chain(H2 * (waves[rows, :] + SHIFT), PTS)
-            ratio = [None] + [ps[m] / ps[m + 1] for m in range(1, PTS)]
-            for c in range(4):
-                a = ends[i, c]
-                y = [None, KAPPA * x_ref[1, c, rows, lanes] + a]
-                for m in range(2, PTS):
-                    y.append(KAPPA * x_ref[m, c, rows, lanes] + ratio[m - 1] * y[-1])
-                o_ref[0, c, rows, lanes] = a
-                value = ends[i, 4 + c]
-                for m in range(PTS - 1, 0, -1):
-                    value = ratio[m] * (y[m] + value)
-                    o_ref[m, c, rows, lanes] = value
-
-    @pl.when(core == 0)
-    def _():
-        tile(0, own_ref, q_ref)
-        tile(1, r_ref, qo_ref)
-
-    @pl.when(core != 0)
-    def _():
-        tile(0, r_ref, qo_ref)
-        tile(1, own_ref, q_ref)
+    chunks = sems.shape[0]
+    per = GRP // chunks
+
+    def half(i, lanes, ends, waves):
+        rows = pl.ds(pl.multiple_of(8 * i, 8), 8)
+        ps = chain(H2 * (waves[rows, :] + SHIFT), PTS)
+        ratio = [None] + [ps[m] / ps[m + 1] for m in range(1, PTS)]
+        for c in range(4):
+            a = ends[i, c]
+            y = [None, KAPPA * x_ref[1, c, rows, lanes] + a]
+            for m in range(2, PTS):
+                y.append(KAPPA * x_ref[m, c, rows, lanes] + ratio[m - 1] * y[-1])
+            buf[0, c, rows, lanes] = a
+            value = ends[i, 4 + c]
+            for m in range(PTS - 1, 0, -1):
+                value = ratio[m] * (y[m] + value)
+                buf[m, c, rows, lanes] = value
+
+    def copy(g):
+        rows = pl.ds(8 * per * g, 8 * per)
+        return pltpu.make_async_copy(buf.at[:, :, rows, :], o_ref.at[:, :, rows, :], sems.at[g])
+
+    for g in range(chunks):
+        @pl.when(core == 0)
+        def _():
+            @pl.loop(per * g, per * (g + 1))
+            def _(i):
+                half(i, slice(0, 128), own_ref, q_ref)
+                half(i, slice(128, 256), r_ref, qo_ref)
+
+        @pl.when(core != 0)
+        def _():
+            @pl.loop(per * g, per * (g + 1))
+            def _(i):
+                half(i, slice(0, 128), r_ref, qo_ref)
+                half(i, slice(128, 256), own_ref, q_ref)
+
+        copy(g).start()
+    for g in range(chunks):
+        copy(g).wait()
+
+
+def in_vmem(value):
+    return pltpu.with_memory_space_constraint(value, pltpu.VMEM)
+
+
+def local_call(kernel, place, operands, shapes):
+    return pl.pallas_call(
+        kernel,
+        in_specs=[pl.BlockSpec(memory_space=pltpu.SMEM)] + [pl.BlockSpec(memory_space=pltpu.VMEM)] * len(operands),
+        out_specs=[pl.BlockSpec(memory_space=pltpu.VMEM)] * len(shapes),
+        out_shape=[pltpu.VMEM(shape, F32) for shape in shapes],
+        compiler_params=pltpu.CompilerParams(vmem_limit_bytes=8 << 20),
+    )(place, *[in_vmem(v) for v in operands])
 
 
 def on_device(forcing, kx_wave, kz_wave):
@@ -293,8 +316,7 @@
     core_groups = [[2 * k + c for k in range(GRP)] for c in range(2)]
     pairs = [(i, i ^ 1) for i in range(32)]
 
-    other = lax.dynamic_slice_in_dim(forcing, 128 * (1 - core), 128, axis=3)
-    swapped = lax.ppermute(other, "kz", pairs)
+    swapped = lax.ppermute(forcing, "kz", pairs)
 
     part = iz // 8
     kx8 = lax.dynamic_slice_in_dim(kx_wave, 8 * (part // 2), 8).astype(F32)
@@ -308,90 +330,24 @@
         jnp.broadcast_to(payload[None], (32, 8, 128)), both, 0, 0, tiled=True, axis_index_groups=wave_groups
     )
 
-    steps = 4
-    tiles = GRP // steps
-    rows = 8 * tiles
-    tiled = lambda n: pl.BlockSpec((tiles, n, 8, 128), lambda i, s: (i, 0, 0, 0))
-    flat = pl.BlockSpec((rows, 128), lambda i, s: (i, 0))
-    up, mid, q_own, q_oth = pl.pallas_call(
-        moments_kernel,
-        grid_spec=pltpu.PrefetchScalarGridSpec(
-            num_scalar_prefetch=1,
-            grid=(steps,),
-            in_specs=[
-                pl.BlockSpec((32, 8, 128), lambda i, s: (0, 0, 0)),
-                pl.BlockSpec((PTS, 4, rows, 128), lambda i, s: (0, 0, i, s[0])),
-                pl.BlockSpec((PTS, 4, rows, 128), lambda i, s: (0, 0, i, 0)),
-            ],
-            out_specs=[tiled(12), tiled(4), flat, flat],
-        ),
-        out_shape=[
-            jax.ShapeDtypeStruct((GRP, 12, 8, 128), F32),
-            jax.ShapeDtypeStruct((GRP, 4, 8, 128), F32),
-            jax.ShapeDtypeStruct((128, 128), F32),
-            jax.ShapeDtypeStruct((128, 128), F32),
-        ],
-    )(place, waves, forcing, swapped)
-
+    up, mid, q_own, q_oth = local_call(
+        moments_kernel, place, (waves, forcing, swapped), ((GRP, 12, 8, 128), (GRP, 4, 8, 128), (128, 128), (128, 128))
+    )
     blocks = lax.all_to_all(up, "kz", 0, 0, tiled=True, axis_index_groups=core_groups)
-
-    whole = lambda *shape: pl.BlockSpec(shape, lambda i, s: (0,) * len(shape))
-    my_q = pl.BlockSpec((8, 128), lambda i, s: (s[2], 0))
-    message = pl.pallas_call(
-        group_kernel,
-        grid_spec=pltpu.PrefetchScalarGridSpec(
-            num_scalar_prefetch=1,
-            grid=(1,),
-            in_specs=[whole(GRP, 12, 8, 128), my_q],
-            out_specs=whole(8, 12, 8, 128),
-        ),
-        out_shape=jax.ShapeDtypeStruct((8, 12, 8, 128), F32),
-    )(place, blocks, q_own)
-
+    (message,) = local_call(group_kernel, place, (blocks, q_own), ((8, 12, 8, 128),))
     messages = lax.all_to_all(message, "kx", 0, 0, tiled=True)
-
-    ends = pl.pallas_call(
-        solve_kernel,
-        grid_spec=pltpu.PrefetchScalarGridSpec(
-            num_scalar_prefetch=1,
-            grid=(1,),
-            in_specs=[whole(GRP, 12, 8, 128), whole(8, 12, 8, 128), my_q],
-            out_specs=whole(GRP, 8, 8, 128),
-        ),
-        out_shape=jax.ShapeDtypeStruct((GRP, 8, 8, 128), F32),
-    )(place, blocks, messages, q_own)
-
+    (ends,) = local_call(solve_kernel, place, (blocks, messages, q_own), ((GRP, 8, 8, 128),))
     ends = lax.all_to_all(ends, "kz", 0, 0, tiled=True, axis_index_groups=core_groups)
-
-    own, send = pl.pallas_call(
-        middle_kernel,
-        grid_spec=pltpu.PrefetchScalarGridSpec(
-            num_scalar_prefetch=1,
-            grid=(steps,),
-            in_specs=[tiled(8), tiled(4), flat],
-            out_specs=[tiled(8), tiled(8)],
-        ),
-        out_shape=[jax.ShapeDtypeStruct((GRP, 8, 8, 128), F32)] * 2,
-    )(place, ends, mid, q_own)
-
+    own, send = local_call(middle_kernel, place, (ends, mid, q_own), ((GRP, 8, 8, 128),) * 2)
     received = lax.ppermute(send, "kz", pairs)
-
     return pl.pallas_call(
         points_kernel,
-        grid_spec=pltpu.PrefetchScalarGridSpec(
-            num_scalar_prefetch=1,
-            grid=(steps,),
-            in_specs=[
-                pl.BlockSpec((PTS, 4, rows, 256), lambda i, s: (0, 0, i, 0)),
-                tiled(8),
-                tiled(8),
-                flat,
-                flat,
-            ],
-            out_specs=pl.BlockSpec((PTS, 4, rows, 256), lambda i, s: (0, 0, i, 0)),
-        ),
+        in_specs=[pl.BlockSpec(memory_space=pltpu.SMEM)] + [pl.BlockSpec(memory_space=pltpu.VMEM)] * 5,
+        out_specs=pl.BlockSpec(memory_space=pl.ANY),
         out_shape=jax.ShapeDtypeStruct(forcing.shape, F32),
-    )(place, forcing, own, received, q_own, q_oth)
+        scratch_shapes=[pltpu.VMEM(forcing.shape, F32), pltpu.SemaphoreType.DMA((4,))],
+        compiler_params=pltpu.CompilerParams(vmem_limit_bytes=8 << 20),
+    )(place, *[in_vmem(v) for v in (forcing, own, received, q_own, q_oth)])
 
 
 def solution(mesh):

time: 118 us -> 101 us (0.86)
  Pallas kernels: 19.9 us -> 6.69 us
  local copies, waits for them, and re-layouts: 4.88 us -> 2.66 us
  blocking collectives: 58.8 us -> 57.5 us
    pallas_call x5, Pallas kernels: 19.9 us -> 6.69 us  [the longest x4 4.26 us: local_call(): pl.pallas_call(kernel, in_specs=[pl.BlockSpec(memory_space=pltpu.SMEM)] +...]
    all_to_all x1, blocking collectives: 12.8 us -> 11.1 us  [on_device(): messages = lax.all_to_all(message, 'kx', 0, 0, tiled=True)]
    dynamic_slice x1 -> x0, local copies, waits for them, and re-layouts: 1.54 us -> none  [on_device(): other = lax.dynamic_slice_in_dim(forcing, 128 * (1 - core), 128, axis=3)]
    unnamed x10 -> x4, local copies, waits for them, and re-layouts: 2.58 us -> 1.89 us
  transfers between devices with their start and end apart: 3 -> 3, of which waited for: 2 -> 2; matrix products, arithmetic and copies ran while one was open for 1% -> 2% of each run, Pallas kernels for 0% -> 0%
where the time goes in v1:
time: 101 us
  blocking collectives  57.5 us (57%)
  starting transfers between devices  19.6 us (19%)
  waiting for transfers between devices  12.8 us (13%)
  Pallas kernels  6.69 us (7%)
  local copies, waits for them, and re-layouts  2.66 us (3%)
  other arithmetic  1.56 us (2%)
    all_to_all x1, blocking collectives, on_device(): lax.all_to_all(up, 'kz', 0, 0, tiled=True, axis_index_groups=core_groups)  26 us
    all_to_all x1, blocking collectives, on_device(): lax.all_to_all(ends, 'kz', 0, 0, tiled=True, axis_index_groups=core_groups)  20.4 us
    all_to_all x1, starting transfers between devices, on_device(): lax.all_to_all(jnp.broadcast_to(payload[None], (32, 8, 128)), both, 0, 0,...  11.9 us
    all_to_all x1, waiting for transfers between devices, on_device(): lax.all_to_all(jnp.broadcast_to(payload[None], (32, 8, 128)), both, 0, 0,...  11.2 us
    all_to_all x1, blocking collectives, on_device(): messages = lax.all_to_all(message, 'kx', 0, 0, tiled=True)  11.1 us
    ppermute x1, starting transfers between devices, on_device(): received = lax.ppermute(send, 'kz', pairs)  4.43 us
    pallas_call x4, Pallas kernels, local_call(): pl.pallas_call(kernel, in_specs=[pl.BlockSpec(memory_space=pltpu.SMEM)] +...  4.26 us
    ppermute x1, starting transfers between devices, on_device(): swapped = lax.ppermute(forcing, 'kz', pairs)  3.24 us
  transfers between devices with their start and end apart: 3, of which 2 were waited for; matrix products, arithmetic and copies ran while one was open for 2% of the time, Pallas kernels for 0%

profile of v1, /device:TPU:1, one launch (start us, length us, event | category | flops | bytes accessed | tf_op | source)
XLA Modules:
  0.0 100.8 jit_solution(16741637171259285995)
XLA Ops:
  0.0 3.2 %collective-permute-start = (f32[6,4,128,256]{3,2,1,0:T(8,128)}, f32[6,4,128,256]{3,2,1,0:T(8,128)S(1)}, u32[]{:S(2)}, u32[]{:S(2)}) collective-permute-start(f32[6,4,128,256]{3,2,1,0:T(8,128)} %x_ref.3), channel_id=1, source_target_pairs={{0,1},{1,0},{2,3},{3,2},{4,5},{5,4},{6,7},{7,6},{8,9},{9,8},{10,11... | collective-permute-start | bytes 9437192 | tf_op jit(solution)/shard_map/ppermute | solution.py:319
  3.2 0.7 convert_element_type.7
  3.9 0.1 broadcast_in_dim.9
  4.0 0.7 iota_shift-right-logical_fusion
  4.8 0.1 fusion
  4.8 0.7 broadcast_in_dim.22
  5.5 11.9 %all-to-all-start = ((f32[32,8,128]{2,1,0:T(8,128)}), f32[32,8,128]{2,1,0:T(8,128)S(1)}, u32[]{:S(2)}, u32[]{:S(2)}) async-start(f32[32,8,128]{2,1,0:T(8,128)} %broadcast_in_dim.22), calls=%async_computation | async-start | bytes 262144 | tf_op jit(solution)/shard_map/all_to_all | solution.py:329
  17.5 0.1 pad_add_fusion.s_ref
  17.5 11.2 %all-to-all-done.w_ref = f32[32,8,128]{2,1,0:T(8,128)S(1)} async-done(((f32[32,8,128]{2,1,0:T(8,128)}), f32[32,8,128]{2,1,0:T(8,128)S(1)}, u32[]{:S(2)}, u32[]{:S(2)}) %all-to-all-start) | async-done | bytes 131104 | tf_op jit(solution)/shard_map/all_to_all | solution.py:329
  28.8 0.0 collective-permute-done.r_ref
  28.8 0.0 copy-start
  28.8 1.9 %copy-done = f32[6,4,128,256]{3,2,1,0:T(8,128)S(1)} copy-done((f32[6,4,128,256]{3,2,1,0:T(8,128)S(1)}, f32[6,4,128,256]{3,2,1,0:T(8,128)}, u32[]{:S(2)}) %copy-start) | copy-done | bytes 3145752
  30.7 1.6 %shard_map.37 = (f32[16,12,8,128]{3,2,1,0:T(8,128)S(1)}, f32[16,4,8,128]{3,2,1,0:T(8,128)S(1)}, f32[128,128]{1,0:T(8,128)S(1)}, f32[128,128]{1,0:T(8,128)S(1)}) custom-call(s32[4]{0:T(128)S(1)} %pad_add_fusion.s_ref, f32[32,8,128]{2,1,0:T(8,128)S(1)} %all-to-all-done.w_ref, f32[6,4,128,256]{3,2,1,0:T(8,128)S(1)} %copy-done, ...), custom_call_target="tpu_custom_call" | custom-call | tf_op jit(solution)/shard_map/pallas_call | solution.py:296
  32.2 26.0 %all_to_all.20.m_ref = f32[16,12,8,128]{3,2,1,0:T(8,128)S(1)} all-to-all(f32[16,12,8,128]{3,2,1,0:T(8,128)S(1)} %get-tuple-element.11), channel_id=1, replica_groups={{0,2,4,6,8,10,12,14,16,18,20,22,24,26,28,30},{1,3,5,7,9,11,13,15,17,19,..., dimensions={0} | all-to-all | bytes 1572864 | tf_op jit(solution)/shard_map/all_to_all | solution.py:336
  58.2 0.0 copy-start.1
  58.2 0.7 shard_map.38
  58.9 11.1 %all_to_all.21.g_ref = f32[8,12,8,128]{3,2,1,0:T(8,128)S(1)} all-to-all(f32[8,12,8,128]{3,2,1,0:T(8,128)S(1)} %shard_map.38), channel_id=1, replica_groups=mesh['kx'=8,'kz'=32] {'kx'}, dimensions={0} | all-to-all | bytes 786432 | tf_op jit(solution)/shard_map/all_to_all | solution.py:338
  70.0 0.7 shard_map.39
  70.7 20.4 %all_to_all.22.b_ref = f32[16,8,8,128]{3,2,1,0:T(8,128)S(1)} all-to-all(f32[16,8,8,128]{3,2,1,0:T(8,128)S(1)} %shard_map.39), channel_id=1, replica_groups={{0,2,4,6,8,10,12,14,16,18,20,22,24,26,28,30},{1,3,5,7,9,11,13,15,17,19,..., dimensions={0} | all-to-all | bytes 1048576 | tf_op jit(solution)/shard_map/all_to_all | solution.py:340
  91.1 1.3 %shard_map.40 = (f32[16,8,8,128]{3,2,1,0:T(8,128)S(1)}, f32[16,8,8,128]{3,2,1,0:T(8,128)S(1)}) custom-call(s32[4]{0:T(128)S(1)} %pad_add_fusion.s_ref, f32[16,8,8,128]{3,2,1,0:T(8,128)S(1)} %all_to_all.22.b_ref, f32[16,4,8,128]{3,2,1,0:T(8,128)S(1)} %get-tuple-element.13.mid_ref, f32[128,128]{1,0:T(8,128)S(1)} %get-tuple-element.12.q_ref), custom_call_target="tpu_custom_call" | custom-call | tf_op jit(solution)/shard_map/pallas_call | solution.py:296
  92.4 4.4 %collective-permute-start.1 = (f32[16,8,8,128]{3,2,1,0:T(8,128)S(1)}, f32[16,8,8,128]{3,2,1,0:T(8,128)S(1)}, u32[]{:S(2)}, u32[]{:S(2)}) collective-permute-start(f32[16,8,8,128]{3,2,1,0:T(8,128)S(1)} %get-tuple-element.15), channel_id=1, source_target_pairs={{0,1},{1,0},{2,3},{3,2},{4,5},{5,4},{6,7},{7,6},{8,9},{9,8},{10,11... | collective-permute-start | bytes 1572872 | tf_op jit(solution)/shard_map/ppermute | solution.py:342
  96.9 1.5 %collective-permute-done.1.r_ref = f32[16,8,8,128]{3,2,1,0:T(8,128)S(1)} collective-permute-done((f32[16,8,8,128]{3,2,1,0:T(8,128)S(1)}, f32[16,8,8,128]{3,2,1,0:T(8,128)S(1)}, u32[]{:S(2)}, u32[]{:S(2)}) %collective-permute-start.1) | collective-permute-done | bytes 524320 | tf_op jit(solution)/shard_map/ppermute | solution.py:342
  98.4 0.0 copy-done.1
  98.4 2.4 %shard_map.41 = f32[6,4,128,256]{3,2,1,0:T(8,128)} custom-call(s32[4]{0:T(128)S(1)} %pad_add_fusion.s_ref, f32[6,4,128,256]{3,2,1,0:T(8,128)S(1)} %copy-done.1, f32[16,8,8,128]{3,2,1,0:T(8,128)S(1)} %get-tuple-element.14.own_ref, f32[16,8,8,128]{3,2,1,0:T(8,128)S(1)} %collective-permute-done.1.r_ref, f32[128,128]{1,0:T(8,128)S(1)} %get-tuple-element.12.q_ref, ...), custom_call_target="tpu_custom_call" | custom-call | tf_op jit(solution)/shard_map/pallas_call | solution.py:343
  (3 shorter events, 0.0 us)
Async XLA Ops:
  0.0 28.8 %collective-permute-start = (f32[6,4,128,256]{3,2,1,0:T(8,128)}, f32[6,4,128,256]{3,2,1,0:T(8,128)S(1)}, u32[]{:S(2)}, u32[]{:S(2)}) collective-permute-start(f32[6,4,128,256]{3,2,1,0:T(8,128)} %x_ref.3), channel_id=1, source_target_pairs={{0,1},{1,0},{2,3},{3,2},{4,5},{5,4},{6,7},{7,6},{8,9},{9,8},{10,11... | collective-permute-start | bytes 9437192 | tf_op jit(solution)/shard_map/ppermute | solution.py:319
  5.5 23.3 %all-to-all-start = ((f32[32,8,128]{2,1,0:T(8,128)}), f32[32,8,128]{2,1,0:T(8,128)S(1)}, u32[]{:S(2)}, u32[]{:S(2)}) async-start(f32[32,8,128]{2,1,0:T(8,128)} %broadcast_in_dim.22), calls=%async_computation | async-start | bytes 262144 | tf_op jit(solution)/shard_map/all_to_all | solution.py:329
  28.8 1.9 %copy-start = (f32[6,4,128,256]{3,2,1,0:T(8,128)S(1)}, f32[6,4,128,256]{3,2,1,0:T(8,128)}, u32[]{:S(2)}) copy-start(f32[6,4,128,256]{3,2,1,0:T(8,128)} %x_ref.3) | copy-start | bytes 9437188
  58.2 40.2 %copy-start.1 = (f32[6,4,128,256]{3,2,1,0:T(8,128)S(1)}, f32[6,4,128,256]{3,2,1,0:T(8,128)}, u32[]{:S(2)}) copy-start(f32[6,4,128,256]{3,2,1,0:T(8,128)} %x_ref.3) | copy-start | bytes 9437188
  92.4 6.0 %collective-permute-start.1 = (f32[16,8,8,128]{3,2,1,0:T(8,128)S(1)}, f32[16,8,8,128]{3,2,1,0:T(8,128)S(1)}, u32[]{:S(2)}, u32[]{:S(2)}) collective-permute-start(f32[16,8,8,128]{3,2,1,0:T(8,128)S(1)} %get-tuple-element.15), channel_id=1, source_target_pairs={{0,1},{1,0},{2,3},{3,2},{4,5},{5,4},{6,7},{7,6},{8,9},{9,8},{10,11... | collective-permute-start | bytes 1572872 | tf_op jit(solution)/shard_map/ppermute | solution.py:342

commit v2 on v1

--- a/solution.py
+++ b/solution.py
@@ -1,3 +1,5 @@
+import functools
+
 import jax
 import jax.numpy as jnp
 from jax import lax
@@ -18,6 +20,12 @@
 F32 = jnp.float32
 
 
+def position():
+    ix = lax.axis_index("kx")
+    iz = lax.axis_index("kz")
+    return lax.rem(iz, 2), ix, lax.div(iz, 2), lax.rem(iz - ix + 32, 8)
+
+
 def chain(eps, n):
     p = [None, jnp.ones_like(eps)]
     diff = 1.0 + eps
@@ -33,9 +41,45 @@
     return jnp.sqrt(eps) * series
 
 
-def moments_kernel(s_ref, w_ref, x_ref, r_ref, up_ref, mid_ref, q_ref, qo_ref):
-    core = s_ref[0]
-    turn = s_ref[3]
+def waves_kernel(kx_hbm, kz_hbm, o_ref, kx_ref, kz_ref, sems):
+    copies = [
+        pltpu.make_async_copy(kx_hbm, kx_ref, sems.at[0]),
+        pltpu.make_async_copy(kz_hbm, kz_ref, sems.at[1]),
+    ]
+    for copy in copies:
+        copy.start()
+    for copy in copies:
+        copy.wait()
+    part = lax.div(lax.axis_index("kz"), 8)
+    sub = lax.broadcasted_iota(jnp.int32, (8, 128), 0)
+    lane = lax.rem(lax.broadcasted_iota(jnp.int32, (8, 128), 1), 8)
+    kx = jnp.zeros((8, 128), jnp.int32)
+    kz = jnp.zeros((8, 128), jnp.int32)
+    for r in range(8):
+        kx = jnp.where(sub == r, jnp.where(part < 2, kx_ref[r], kx_ref[8 + r]), kx)
+        kz = jnp.where(lane == r, kz_ref[r], kz)
+    row = jnp.where(lax.div(sub, 4) == lax.rem(part, 2), kx, kz).astype(F32)
+    for j in range(o_ref.shape[0]):
+        o_ref[j] = row
+
+
+def moments_kernel(w_ref, x_ref, r_ref, up_ref, mid_ref, q_ref, qo_ref, ratio_ref, x_own, sems):
+    core, _, _, turn = position()
+    chunks = sems.shape[0]
+    per = GRP // chunks
+
+    def copy(g, half):
+        rows = pl.ds(8 * per * g, 8 * per)
+        return pltpu.make_async_copy(
+            x_ref.at[:, :, rows, pl.ds(128 * half, 128)], x_own.at[:, :, rows, :], sems.at[g]
+        )
+
+    for half in range(2):
+        @pl.when(core == half)
+        def _():
+            for g in range(chunks):
+                copy(g, half).start()
+
     lane = lax.broadcasted_iota(jnp.int32, (8, 128), 1) // 8
     sub = lax.broadcasted_iota(jnp.int32, (8, 128), 0)
 
@@ -50,8 +94,8 @@
     kz_own = kz_row(core)
     kz_oth = kz_row(1 - core)
 
-    def tiles(first, second):
-        @pl.loop(0, GRP)
+    def tiles(g, first, second):
+        @pl.loop(per * g, per * (g + 1), unroll=2)
         def _(i):
             kx = (ALPHA_X * jnp.where(sub < 4, w_ref[2 * i], w_ref[2 * i + 1])) ** 2
             rows = pl.ds(pl.multiple_of(8 * i, 8), 8)
@@ -60,6 +104,8 @@
             qo_ref[rows, :] = kx + kz_oth
             ps = chain(H2 * (q + SHIFT), BLK)
             pq = chain(H2 * q, BLK)
+            ratio = ps[PTS] / ps[BLK]
+            ratio_ref[rows, :] = ratio
             for c in range(4):
                 f = [first(m, c, rows) for m in range(PTS)] + [second(m, c, rows) for m in range(PTS)]
                 own = ps[BLK] * f[0]
@@ -72,7 +118,7 @@
                     mid = mid + ps[min(m, BLK - m)] * f[m]
                 up_ref[i, c] = KAPPA * own
                 up_ref[i, 4 + c] = KAPPA * nxt
-                mid_ref[i, c] = KAPPA * mid
+                mid_ref[i, c] = ratio * (KAPPA * mid)
                 if c < 2:
                     own = pq[BLK] * f[0]
                     nxt = pq[1] * f[1]
@@ -83,13 +129,16 @@
                     up_ref[i, 8 + c] = KAPPA * own
                     up_ref[i, 10 + c] = KAPPA * nxt
 
-    @pl.when(core == 0)
-    def _():
-        tiles(lambda m, c, rows: x_ref[m, c, rows, :128], lambda m, c, rows: r_ref[m, c, rows, :128])
-
-    @pl.when(core != 0)
-    def _():
-        tiles(lambda m, c, rows: r_ref[m, c, rows, 128:], lambda m, c, rows: x_ref[m, c, rows, 128:])
+    for g in range(chunks):
+        copy(g, 0).wait()
+
+        @pl.when(core == 0)
+        def _():
+            tiles(g, lambda m, c, rows: x_own[m, c, rows, :], lambda m, c, rows: r_ref[m, c, rows, :128])
+
+        @pl.when(core != 0)
+        def _():
+            tiles(g, lambda m, c, rows: r_ref[m, c, rows, 128:], lambda m, c, rows: x_own[m, c, rows, :])
 
 
 def sources(m_ref, own, nxt):
@@ -100,9 +149,9 @@
     )
 
 
-def group_kernel(s_ref, m_ref, q_ref, o_ref):
-    group = s_ref[1]
-    q = q_ref[pl.ds(pl.multiple_of(8 * s_ref[2], 8), 8), :]
+def group_kernel(m_ref, q_ref, o_ref):
+    _, group, chip, _ = position()
+    q = q_ref[pl.ds(pl.multiple_of(8 * chip, 8), 8), :]
     rho = jnp.exp(-BLK * angle(H2 * (q + SHIFT)))
     res = [None] * 12
     for c in range(4):
@@ -136,10 +185,10 @@
             o_ref[k, n] = res[n]
 
 
-def solve_kernel(s_ref, m_ref, g_ref, q_ref, o_ref):
-    group = s_ref[1]
+def solve_kernel(m_ref, g_ref, q_ref, o_ref):
+    _, group, chip, _ = position()
     groups = g_ref.shape[0]
-    q = q_ref[pl.ds(pl.multiple_of(8 * s_ref[2], 8), 8), :]
+    q = q_ref[pl.ds(pl.multiple_of(8 * chip, 8), 8), :]
     es = H2 * (q + SHIFT)
     eq = H2 * q
     ts = angle(es)
@@ -218,18 +267,17 @@
                 o_ref[d - 1, 4 + c] = value
 
 
-def middle_kernel(s_ref, b_ref, mid_ref, q_ref, own_ref, send_ref):
-    core = s_ref[0]
+def middle_kernel(b_ref, mid_ref, ratio_ref, own_ref, send_ref):
+    core, _, _, _ = position()
 
     def tiles(lower, upper):
-        @pl.loop(0, GRP)
+        @pl.loop(0, GRP, unroll=2)
         def _(i):
-            ps = chain(H2 * (q_ref[pl.ds(pl.multiple_of(8 * i, 8), 8), :] + SHIFT), BLK)
-            ratio = ps[PTS] / ps[BLK]
+            ratio = ratio_ref[pl.ds(pl.multiple_of(8 * i, 8), 8), :]
             for c in range(4):
                 a = b_ref[i, c]
                 b = b_ref[i, 4 + c]
-                x = ratio * (a + b + mid_ref[i, c])
+                x = ratio * (a + b) + mid_ref[i, c]
                 lower[i, c] = a
                 lower[i, 4 + c] = x
                 upper[i, c] = x
@@ -244,71 +292,62 @@
         tiles(send_ref, own_ref)
 
 
-def points_kernel(s_ref, x_ref, own_ref, r_ref, q_ref, qo_ref, o_ref, buf, sems):
-    core = s_ref[0]
+def points_kernel(other, x_ref, ends, q_ref, *refs):
+    o_ref, buf, sems = refs[-3:]
+    core, _, _, _ = position()
     chunks = sems.shape[0]
     per = GRP // chunks
 
-    def half(i, lanes, ends, waves):
+    def tile(i, lanes):
         rows = pl.ds(pl.multiple_of(8 * i, 8), 8)
-        ps = chain(H2 * (waves[rows, :] + SHIFT), PTS)
+        ps = chain(H2 * (q_ref[rows, :] + SHIFT), PTS)
         ratio = [None] + [ps[m] / ps[m + 1] for m in range(1, PTS)]
         for c in range(4):
             a = ends[i, c]
             y = [None, KAPPA * x_ref[1, c, rows, lanes] + a]
             for m in range(2, PTS):
                 y.append(KAPPA * x_ref[m, c, rows, lanes] + ratio[m - 1] * y[-1])
-            buf[0, c, rows, lanes] = a
+            buf[0, c, rows, :] = a
             value = ends[i, 4 + c]
             for m in range(PTS - 1, 0, -1):
                 value = ratio[m] * (y[m] + value)
-                buf[m, c, rows, lanes] = value
-
-    def copy(g):
+                buf[m, c, rows, :] = value
+
+    def copy(g, half):
         rows = pl.ds(8 * per * g, 8 * per)
-        return pltpu.make_async_copy(buf.at[:, :, rows, :], o_ref.at[:, :, rows, :], sems.at[g])
+        return pltpu.make_async_copy(
+            buf.at[:, :, rows, :], o_ref.at[:, :, rows, pl.ds(128 * half, 128)], sems.at[g]
+        )
+
+    for half in range(2):
+        @pl.when(core == (1 - half if other else half))
+        def _():
+            for g in range(chunks):
+                @pl.loop(per * g, per * (g + 1), unroll=2)
+                def _(i):
+                    tile(i, slice(128 * half, 128 * half + 128))
+
+                copy(g, half).start()
 
     for g in range(chunks):
-        @pl.when(core == 0)
-        def _():
-            @pl.loop(per * g, per * (g + 1))
-            def _(i):
-                half(i, slice(0, 128), own_ref, q_ref)
-                half(i, slice(128, 256), r_ref, qo_ref)
-
-        @pl.when(core != 0)
-        def _():
-            @pl.loop(per * g, per * (g + 1))
-            def _(i):
-                half(i, slice(0, 128), r_ref, qo_ref)
-                half(i, slice(128, 256), own_ref, q_ref)
-
-        copy(g).start()
-    for g in range(chunks):
-        copy(g).wait()
+        copy(g, 0).wait()
 
 
 def in_vmem(value):
     return pltpu.with_memory_space_constraint(value, pltpu.VMEM)
 
 
-def local_call(kernel, place, operands, shapes):
+def local_call(kernel, operands, shapes):
     return pl.pallas_call(
         kernel,
-        in_specs=[pl.BlockSpec(memory_space=pltpu.SMEM)] + [pl.BlockSpec(memory_space=pltpu.VMEM)] * len(operands),
+        in_specs=[pl.BlockSpec(memory_space=pltpu.VMEM)] * len(operands),
         out_specs=[pl.BlockSpec(memory_space=pltpu.VMEM)] * len(shapes),
         out_shape=[pltpu.VMEM(shape, F32) for shape in shapes],
         compiler_params=pltpu.CompilerParams(vmem_limit_bytes=8 << 20),
-    )(place, *[in_vmem(v) for v in operands])
+    )(*[in_vmem(v) for v in operands])
 
 
 def on_device(forcing, kx_wave, kz_wave):
-    ix = lax.axis_index("kx")
-    iz = lax.axis_index("kz")
-    core = lax.rem(iz, 2)
-    chip = iz // 2
-    turn = lax.rem(iz - ix + 32, 8)
-    place = jnp.stack([core, ix, chip, turn]).astype(jnp.int32)
     both = ("kx", "kz")
     wave_groups = [
         [k * 32 + (k + t) % 8 + 8 * part for k in range(8) for part in range(4)] for t in range(8)
@@ -316,38 +355,59 @@
     core_groups = [[2 * k + c for k in range(GRP)] for c in range(2)]
     pairs = [(i, i ^ 1) for i in range(32)]
 
+    vmem = pl.BlockSpec(memory_space=pltpu.VMEM)
+    hbm = pl.BlockSpec(memory_space=pltpu.HBM)
+    params = pltpu.CompilerParams(vmem_limit_bytes=8 << 20)
+    half_shape = (PTS, 4, 128, 128)
+
     swapped = lax.ppermute(forcing, "kz", pairs)
 
-    part = iz // 8
-    kx8 = lax.dynamic_slice_in_dim(kx_wave, 8 * (part // 2), 8).astype(F32)
-    sub = lax.broadcasted_iota(jnp.int32, (8, 128), 0)
-    payload = jnp.where(
-        sub // 4 == lax.rem(part, 2),
-        jnp.broadcast_to(kx8[:, None], (8, 128)),
-        jnp.broadcast_to(jnp.tile(kz_wave.astype(F32), 16)[None, :], (8, 128)),
-    )
-    waves = lax.all_to_all(
-        jnp.broadcast_to(payload[None], (32, 8, 128)), both, 0, 0, tiled=True, axis_index_groups=wave_groups
-    )
-
-    up, mid, q_own, q_oth = local_call(
-        moments_kernel, place, (waves, forcing, swapped), ((GRP, 12, 8, 128), (GRP, 4, 8, 128), (128, 128), (128, 128))
-    )
+    payload = pl.pallas_call(
+        waves_kernel,
+        in_specs=[hbm] * 2,
+        out_specs=vmem,
+        out_shape=pltpu.VMEM((32, 8, 128), F32),
+        scratch_shapes=[
+            pltpu.SMEM(kx_wave.shape, jnp.int32),
+            pltpu.SMEM(kz_wave.shape, jnp.int32),
+            pltpu.SemaphoreType.DMA((2,)),
+        ],
+        compiler_params=params,
+    )(*[pltpu.with_memory_space_constraint(v, pltpu.HBM) for v in (kx_wave, kz_wave)])
+    waves = lax.all_to_all(payload, both, 0, 0, tiled=True, axis_index_groups=wave_groups)
+    up, mid, q_own, q_oth, ratio = pl.pallas_call(
+        moments_kernel,
+        in_specs=[vmem, hbm, vmem],
+        out_specs=[vmem] * 5,
+        out_shape=[
+            pltpu.VMEM(shape, F32)
+            for shape in ((GRP, 12, 8, 128), (GRP, 4, 8, 128), (128, 128), (128, 128), (128, 128))
+        ],
+        scratch_shapes=[pltpu.VMEM(half_shape, F32), pltpu.SemaphoreType.DMA((4,))],
+        compiler_params=params,
+    )(in_vmem(waves), pltpu.with_memory_space_constraint(forcing, pltpu.HBM), in_vmem(swapped))
     blocks = lax.all_to_all(up, "kz", 0, 0, tiled=True, axis_index_groups=core_groups)
-    (message,) = local_call(group_kernel, place, (blocks, q_own), ((8, 12, 8, 128),))
+    (message,) = local_call(group_kernel, (blocks, q_own), ((8, 12, 8, 128),))
     messages = lax.all_to_all(message, "kx", 0, 0, tiled=True)
-    (ends,) = local_call(solve_kernel, place, (blocks, messages, q_own), ((GRP, 8, 8, 128),))
+    (ends,) = local_call(solve_kernel, (blocks, messages, q_own), ((GRP, 8, 8, 128),))
     ends = lax.all_to_all(ends, "kz", 0, 0, tiled=True, axis_index_groups=core_groups)
-    own, send = local_call(middle_kernel, place, (ends, mid, q_own), ((GRP, 8, 8, 128),) * 2)
+    own, send = local_call(middle_kernel, (ends, mid, ratio), ((GRP, 8, 8, 128),) * 2)
     received = lax.ppermute(send, "kz", pairs)
-    return pl.pallas_call(
-        points_kernel,
-        in_specs=[pl.BlockSpec(memory_space=pltpu.SMEM)] + [pl.BlockSpec(memory_space=pltpu.VMEM)] * 5,
-        out_specs=pl.BlockSpec(memory_space=pl.ANY),
-        out_shape=jax.ShapeDtypeStruct(forcing.shape, F32),
-        scratch_shapes=[pltpu.VMEM(forcing.shape, F32), pltpu.SemaphoreType.DMA((4,))],
-        compiler_params=pltpu.CompilerParams(vmem_limit_bytes=8 << 20),
-    )(place, *[in_vmem(v) for v in (forcing, own, received, q_own, q_oth)])
+
+    def points(other, operands, *made):
+        return pl.pallas_call(
+            functools.partial(points_kernel, other),
+            in_specs=[vmem] * 3 + [hbm] * len(made),
+            out_specs=hbm,
+            out_shape=pltpu.HBM(forcing.shape, F32),
+            input_output_aliases={3: 0} if made else {},
+            scratch_shapes=[pltpu.VMEM(half_shape, F32), pltpu.SemaphoreType.DMA((4,))],
+            compiler_params=params,
+            cost_estimate=pl.CostEstimate(flops=8 << 20, bytes_accessed=4 << 20, transcendentals=0),
+        )(*[in_vmem(v) for v in operands], *made)
+
+    fields = points(False, (forcing, own, q_own))
+    return points(True, (forcing, received, q_oth), fields)
 
 
 def solution(mesh):

time: 101 us -> 94.5 us (0.936)
  blocking collectives: 57.5 us -> 80.7 us
  waiting for transfers between devices: 12.8 us -> 0.26 us
  starting transfers between devices: 19.6 us -> 7.68 us
  local copies, waits for them, and re-layouts: 2.66 us -> 0.01 us
  other arithmetic: 1.56 us -> 0 us
  Pallas kernels: 6.69 us -> 5.64 us
    all_to_all x0 -> x1, blocking collectives: none -> 23.1 us  [on_device(): lax.all_to_all(payload, both, 0, 0, tiled=True, axis_index_groups=wave_gr...]
    all_to_all x1 -> x0, starting transfers between devices: 11.9 us -> none  [on_device(): lax.all_to_all(jnp.broadcast_to(payload[None], (32, 8, 128)), both, 0, 0,...]
    all_to_all x1 -> x0, waiting for transfers between devices: 11.2 us -> none  [on_device(): lax.all_to_all(jnp.broadcast_to(payload[None], (32, 8, 128)), both, 0, 0,...]
    unnamed x4 -> x2, local copies, waits for them, and re-layouts: 1.89 us -> 0.01 us
    ppermute x1, waiting for transfers between devices: 1.54 us -> 0.26 us  [on_device(): received = lax.ppermute(send, 'kz', pairs)]
    pallas_call x5 -> x7, Pallas kernels: 6.69 us -> 5.64 us  [the longest x2 2.53 us: points(): pl.pallas_call(functools.partial(points_kernel, other), in_specs=[vmem] *...]
  transfers between devices with their start and end apart: 3 -> 2, of which waited for: 2 -> 1; matrix products, arithmetic and copies ran while one was open for 2% -> 0% of each run, Pallas kernels for 0% -> 2%
where the time goes in v2:
time: 94.5 us; the launch traced here: 94.3 us
  blocking collectives  80.7 us (85%)
  starting transfers between devices  7.68 us (8%)
  Pallas kernels  5.64 us (6%)
    all_to_all x1, blocking collectives, on_device(): lax.all_to_all(up, 'kz', 0, 0, tiled=True, axis_index_groups=core_groups)  26 us
    all_to_all x1, blocking collectives, on_device(): lax.all_to_all(payload, both, 0, 0, tiled=True, axis_index_groups=wave_gr...  23.1 us
    all_to_all x1, blocking collectives, on_device(): lax.all_to_all(ends, 'kz', 0, 0, tiled=True, axis_index_groups=core_groups)  20.5 us
    all_to_all x1, blocking collectives, on_device(): messages = lax.all_to_all(message, 'kx', 0, 0, tiled=True)  11.2 us
    ppermute x1, starting transfers between devices, on_device(): received = lax.ppermute(send, 'kz', pairs)  4.44 us
    ppermute x1, starting transfers between devices, on_device(): swapped = lax.ppermute(forcing, 'kz', pairs)  3.24 us
    pallas_call x2, Pallas kernels, points(): pl.pallas_call(functools.partial(points_kernel, other), in_specs=[vmem] *...  2.53 us
    pallas_call x1, Pallas kernels, on_device(): pl.pallas_call(moments_kernel, in_specs=[vmem, hbm, vmem], out_specs=[vme...  1.98 us
  transfers between devices with their start and end apart: 2, of which 1 were waited for; matrix products, arithmetic and copies ran while one was open for 0% of the time, Pallas kernels for 2%

profile of v2, /device:TPU:1, one launch (start us, length us, event | category | flops | bytes accessed | tf_op | source)
XLA Modules:
  0.0 94.3 jit_solution(12314783280283127929)
XLA Ops:
  0.0 3.2 %collective-permute-start = (f32[6,4,128,256]{3,2,1,0:T(8,128)}, f32[6,4,128,256]{3,2,1,0:T(8,128)S(1)}, u32[]{:S(2)}, u32[]{:S(2)}) collective-permute-start(f32[6,4,128,256]{3,2,1,0:T(8,128)} %x_ref.5), channel_id=1, source_target_pairs={{0,1},{1,0},{2,3},{3,2},{4,5},{5,4},{6,7},{7,6},{8,9},{9,8},{10,11... | collective-permute-start | bytes 9437192 | tf_op jit(solution)/shard_map/ppermute | solution.py:363
  3.2 0.7 shard_map.37
  4.0 23.1 %all_to_all.20.w_ref = f32[32,8,128]{2,1,0:T(8,128)S(1)} all-to-all(f32[32,8,128]{2,1,0:T(8,128)S(1)} %shard_map.37), channel_id=1, replica_groups={{0,8,16,24,33,41,49,57,66,74,82,90,99,107,115,123,132,140,148,156,165,1..., dimensions={0} | all-to-all | bytes 262144 | tf_op jit(solution)/shard_map/all_to_all | solution.py:377
  27.0 0.0 collective-permute-done.r_ref
  27.0 2.0 %shard_map.38 = (f32[16,12,8,128]{3,2,1,0:T(8,128)S(1)}, f32[16,4,8,128]{3,2,1,0:T(8,128)S(1)}, f32[128,128]{1,0:T(8,128)S(1)}, f32[128,128]{1,0:T(8,128)S(1)}, f32[128,128]{1,0:T(8,128)S(1)}) custom-call(f32[32,8,128]{2,1,0:T(8,128)S(1)} %all_to_all.20.w_ref, f32[6,4,128,256]{3,2,1,0:T(8,128)} %x_ref.5, f32[6,4,128,256]{3,2,1,0:T(8,128)S(1)} %collective-permute-done.r_ref), custom_call_target="tpu_custom_call" | custom-call | tf_op jit(solution)/shard_map/pallas_call | solution.py:378
  29.0 26.0 %all_to_all.21.m_ref = f32[16,12,8,128]{3,2,1,0:T(8,128)S(1)} all-to-all(f32[16,12,8,128]{3,2,1,0:T(8,128)S(1)} %get-tuple-element.12), channel_id=1, replica_groups={{0,2,4,6,8,10,12,14,16,18,20,22,24,26,28,30},{1,3,5,7,9,11,13,15,17,19,..., dimensions={0} | all-to-all | bytes 1572864 | tf_op jit(solution)/shard_map/all_to_all | solution.py:389
  55.0 0.0 copy-start
  55.0 0.1 shard_map.39
  55.1 11.2 %all_to_all.22.g_ref = f32[8,12,8,128]{3,2,1,0:T(8,128)S(1)} all-to-all(f32[8,12,8,128]{3,2,1,0:T(8,128)S(1)} %shard_map.39), channel_id=1, replica_groups=mesh['kx'=8,'kz'=32] {'kx'}, dimensions={0} | all-to-all | bytes 786432 | tf_op jit(solution)/shard_map/all_to_all | solution.py:391
  66.3 0.2 shard_map.40
  66.5 20.5 %all_to_all.23.b_ref = f32[16,8,8,128]{3,2,1,0:T(8,128)S(1)} all-to-all(f32[16,8,8,128]{3,2,1,0:T(8,128)S(1)} %shard_map.40), channel_id=1, replica_groups={{0,2,4,6,8,10,12,14,16,18,20,22,24,26,28,30},{1,3,5,7,9,11,13,15,17,19,..., dimensions={0} | all-to-all | bytes 1048576 | tf_op jit(solution)/shard_map/all_to_all | solution.py:393
  87.0 0.1 shard_map.41
  87.1 4.4 %collective-permute-start.1 = (f32[16,8,8,128]{3,2,1,0:T(8,128)S(1)}, f32[16,8,8,128]{3,2,1,0:T(8,128)S(1)}, u32[]{:S(2)}, u32[]{:S(2)}) collective-permute-start(f32[16,8,8,128]{3,2,1,0:T(8,128)S(1)} %get-tuple-element.16), channel_id=1, source_target_pairs={{0,1},{1,0},{2,3},{3,2},{4,5},{5,4},{6,7},{7,6},{8,9},{9,8},{10,11... | collective-permute-start | bytes 1572872 | tf_op jit(solution)/shard_map/ppermute | solution.py:395
  91.5 0.0 copy-done
  91.5 1.3 %shard_map.42.refs_0_ = f32[6,4,128,256]{3,2,1,0:T(8,128)} custom-call(f32[6,4,128,256]{3,2,1,0:T(8,128)S(1)} %copy-done, f32[16,8,8,128]{3,2,1,0:T(8,128)S(1)} %get-tuple-element.18.ends, f32[128,128]{1,0:T(8,128)S(1)} %get-tuple-element.13.q_ref), custom_call_target="tpu_custom_call" | custom-call | flops 8388608 | bytes 4194304 | tf_op jit(solution)/shard_map/pallas_call | solution.py:398
  92.8 0.3 collective-permute-done.1.ends
  93.1 1.3 %shard_map.43 = f32[6,4,128,256]{3,2,1,0:T(8,128)} custom-call(f32[6,4,128,256]{3,2,1,0:T(8,128)S(1)} %copy-done, f32[16,8,8,128]{3,2,1,0:T(8,128)S(1)} %collective-permute-done.1.ends, f32[128,128]{1,0:T(8,128)S(1)} %get-tuple-element.17.q_ref, f32[6,4,128,256]{3,2,1,0:T(8,128)} %shard_map.42.refs_0_), custom_call_target="tpu_custom_call", output_to_operand_aliasing={{}: (3, {})} | custom-call | flops 8388608 | bytes 4194304 | tf_op jit(solution)/shard_map/pallas_call | solution.py:398
Async XLA Ops:
  0.0 27.0 %collective-permute-start = (f32[6,4,128,256]{3,2,1,0:T(8,128)}, f32[6,4,128,256]{3,2,1,0:T(8,128)S(1)}, u32[]{:S(2)}, u32[]{:S(2)}) collective-permute-start(f32[6,4,128,256]{3,2,1,0:T(8,128)} %x_ref.5), channel_id=1, source_target_pairs={{0,1},{1,0},{2,3},{3,2},{4,5},{5,4},{6,7},{7,6},{8,9},{9,8},{10,11... | collective-permute-start | bytes 9437192 | tf_op jit(solution)/shard_map/ppermute | solution.py:363
  55.0 36.5 %copy-start = (f32[6,4,128,256]{3,2,1,0:T(8,128)S(1)}, f32[6,4,128,256]{3,2,1,0:T(8,128)}, u32[]{:S(2)}) copy-start(f32[6,4,128,256]{3,2,1,0:T(8,128)} %x_ref.5) | copy-start | bytes 9437188
  87.1 6.0 %collective-permute-start.1 = (f32[16,8,8,128]{3,2,1,0:T(8,128)S(1)}, f32[16,8,8,128]{3,2,1,0:T(8,128)S(1)}, u32[]{:S(2)}, u32[]{:S(2)}) collective-permute-start(f32[16,8,8,128]{3,2,1,0:T(8,128)S(1)} %get-tuple-element.16), channel_id=1, source_target_pairs={{0,1},{1,0},{2,3},{3,2},{4,5},{5,4},{6,7},{7,6},{8,9},{9,8},{10,11... | collective-permute-start | bytes 1572872 | tf_op jit(solution)/shard_map/ppermute | solution.py:395

commit v3 on v2

--- a/solution.py
+++ b/solution.py
@@ -21,9 +21,21 @@
 
 
 def position():
+    iz = lax.axis_index("kz")
+    return lax.rem(iz, 2), lax.axis_index("kx"), lax.div(iz, 2)
+
+
+def wave_group():
     ix = lax.axis_index("kx")
     iz = lax.axis_index("kz")
-    return lax.rem(iz, 2), ix, lax.div(iz, 2), lax.rem(iz - ix + 32, 8)
+    x_lo, y = lax.div(ix, 4), lax.rem(ix, 4)
+    z, x_hi = lax.div(iz, 4), lax.rem(lax.div(iz, 2), 2)
+    return lax.rem(y - z + 8, 4), lax.rem(x_lo + x_hi + lax.div(z, 4), 2)
+
+
+def wave_member(j, ty, tx):
+    x_lo, y, b, core = j // 16, j // 4 % 4, j // 2 % 2, j % 2
+    return 4 * ((y - ty + 4) % 4 + 4 * b) + 2 * ((x_lo + tx + b) % 2) + core
 
 
 def chain(eps, n):
@@ -50,21 +62,23 @@
         copy.start()
     for copy in copies:
         copy.wait()
-    part = lax.div(lax.axis_index("kz"), 8)
-    sub = lax.broadcasted_iota(jnp.int32, (8, 128), 0)
-    lane = lax.rem(lax.broadcasted_iota(jnp.int32, (8, 128), 1), 8)
-    kx = jnp.zeros((8, 128), jnp.int32)
-    kz = jnp.zeros((8, 128), jnp.int32)
+    iz = lax.axis_index("kz")
+    part = 2 * lax.div(iz, 16) + lax.rem(iz, 2)
+    lane = lax.broadcasted_iota(jnp.int32, (2, 128), 1)
+    kx = jnp.zeros((2, 128), jnp.int32)
+    kz = jnp.zeros((2, 128), jnp.int32)
+    for r in range(4):
+        kx = jnp.where(lax.rem(lane, 4) == r, kx_ref[4 * part + r], kx)
     for r in range(8):
-        kx = jnp.where(sub == r, jnp.where(part < 2, kx_ref[r], kx_ref[8 + r]), kx)
-        kz = jnp.where(lane == r, kz_ref[r], kz)
-    row = jnp.where(lax.div(sub, 4) == lax.rem(part, 2), kx, kz).astype(F32)
+        kz = jnp.where(lax.rem(lane, 8) == r, kz_ref[r], kz)
+    rows = jnp.where(lax.broadcasted_iota(jnp.int32, (2, 128), 0) == 0, kz, kx).astype(F32)
     for j in range(o_ref.shape[0]):
-        o_ref[j] = row
+        o_ref[j] = rows
 
 
 def moments_kernel(w_ref, x_ref, r_ref, up_ref, mid_ref, q_ref, qo_ref, ratio_ref, x_own, sems):
-    core, _, _, turn = position()
+    core, _, _ = position()
+    ty, tx = wave_group()
     chunks = sems.shape[0]
     per = GRP // chunks
 
@@ -80,28 +94,34 @@
             for g in range(chunks):
                 copy(g, half).start()
 
-    lane = lax.broadcasted_iota(jnp.int32, (8, 128), 1) // 8
+    lane = lax.broadcasted_iota(jnp.int32, (8, 128), 1)
     sub = lax.broadcasted_iota(jnp.int32, (8, 128), 0)
+    places = [wave_member(j, ty, tx) for j in range(32)]
 
     def kz_row(half):
-        acc = [jnp.zeros((8, 128), F32), jnp.zeros((8, 128), F32)]
+        acc = [jnp.zeros((1, 128), F32) for _ in range(4)]
         for j in range(32):
-            place = lax.rem(j // 4 + turn, 8) + 8 * (j % 4) - GRP * half
-            acc[j % 2] = acc[j % 2] + jnp.where(lane == place, w_ref[j], 0.0)
-        row = acc[0][4:5, :] + acc[1][0:1, :]
+            acc[j % 4] = jnp.where(lane[0:1] // 8 == places[j] - GRP * half, w_ref[j, 0:1, :], acc[j % 4])
+        row = (acc[0] + acc[1]) + (acc[2] + acc[3])
         return (BETA_Z * jnp.broadcast_to(row, (8, 128))) ** 2
+
+    def kx_column(i):
+        rows = jnp.where(sub < 4, w_ref[2 * i, 1:2, :], w_ref[2 * i + 1, 1:2, :])
+        column = jnp.sum(jnp.where(lane == lax.rem(sub, 4), rows, 0.0), axis=1, keepdims=True)
+        return (ALPHA_X * jnp.broadcast_to(column, (8, 128))) ** 2
 
     kz_own = kz_row(core)
     kz_oth = kz_row(1 - core)
+    for i in range(GRP):
+        kx = kx_column(i)
+        q_ref[8 * i : 8 * i + 8, :] = kx + kz_own
+        qo_ref[8 * i : 8 * i + 8, :] = kx + kz_oth
 
     def tiles(g, first, second):
         @pl.loop(per * g, per * (g + 1), unroll=2)
         def _(i):
-            kx = (ALPHA_X * jnp.where(sub < 4, w_ref[2 * i], w_ref[2 * i + 1])) ** 2
             rows = pl.ds(pl.multiple_of(8 * i, 8), 8)
-            q = kx + kz_own
-            q_ref[rows, :] = q
-            qo_ref[rows, :] = kx + kz_oth
+            q = q_ref[rows, :]
             ps = chain(H2 * (q + SHIFT), BLK)
             pq = chain(H2 * q, BLK)
             ratio = ps[PTS] / ps[BLK]
@@ -109,13 +129,14 @@
             for c in range(4):
                 f = [first(m, c, rows) for m in range(PTS)] + [second(m, c, rows) for m in range(PTS)]
                 own = ps[BLK] * f[0]
-                nxt = ps[1] * f[1]
-                mid = ps[1] * f[1]
+                nxt = jnp.zeros_like(own)
+                mid = jnp.zeros_like(own)
                 for m in range(1, BLK):
-                    own = own + ps[BLK - m] * f[m]
-                for m in range(2, BLK):
-                    nxt = nxt + ps[m] * f[m]
-                    mid = mid + ps[min(m, BLK - m)] * f[m]
+                    to_own = ps[BLK - m] * f[m]
+                    to_nxt = ps[m] * f[m]
+                    own = own + to_own
+                    nxt = nxt + to_nxt
+                    mid = mid + (to_nxt if m <= PTS else to_own)
                 up_ref[i, c] = KAPPA * own
                 up_ref[i, 4 + c] = KAPPA * nxt
                 mid_ref[i, c] = ratio * (KAPPA * mid)
@@ -150,7 +171,7 @@
 
 
 def group_kernel(m_ref, q_ref, o_ref):
-    _, group, chip, _ = position()
+    _, group, chip = position()
     q = q_ref[pl.ds(pl.multiple_of(8 * chip, 8), 8), :]
     rho = jnp.exp(-BLK * angle(H2 * (q + SHIFT)))
     res = [None] * 12
@@ -186,7 +207,7 @@
 
 
 def solve_kernel(m_ref, g_ref, q_ref, o_ref):
-    _, group, chip, _ = position()
+    _, group, chip = position()
     groups = g_ref.shape[0]
     q = q_ref[pl.ds(pl.multiple_of(8 * chip, 8), 8), :]
     es = H2 * (q + SHIFT)
@@ -268,7 +289,7 @@
 
 
 def middle_kernel(b_ref, mid_ref, ratio_ref, own_ref, send_ref):
-    core, _, _, _ = position()
+    core, _, _ = position()
 
     def tiles(lower, upper):
         @pl.loop(0, GRP, unroll=2)
@@ -294,7 +315,7 @@
 
 def points_kernel(other, x_ref, ends, q_ref, *refs):
     o_ref, buf, sems = refs[-3:]
-    core, _, _, _ = position()
+    core, _, _ = position()
     chunks = sems.shape[0]
     per = GRP // chunks
 
@@ -350,7 +371,7 @@
 def on_device(forcing, kx_wave, kz_wave):
     both = ("kx", "kz")
     wave_groups = [
-        [k * 32 + (k + t) % 8 + 8 * part for k in range(8) for part in range(4)] for t in range(8)
+        [32 * (j // 4) + wave_member(j, ty, tx) for j in range(32)] for ty in range(4) for tx in range(2)
     ]
     core_groups = [[2 * k + c for k in range(GRP)] for c in range(2)]
     pairs = [(i, i ^ 1) for i in range(32)]
@@ -366,7 +387,7 @@
         waves_kernel,
         in_specs=[hbm] * 2,
         out_specs=vmem,
-        out_shape=pltpu.VMEM((32, 8, 128), F32),
+        out_shape=pltpu.VMEM((32, 2, 128), F32),
         scratch_shapes=[
             pltpu.SMEM(kx_wave.shape, jnp.int32),
             pltpu.SMEM(kz_wave.shape, jnp.int32),

time: 94.5 us -> 93 us (0.984)
  blocking collectives: 80.7 us -> 79.2 us
    all_to_all x1, blocking collectives: 23.1 us -> 21.2 us  [on_device(): lax.all_to_all(payload, both, 0, 0, tiled=True, axis_index_groups=wave_gr...]
    all_to_all x1, blocking collectives: 26 us -> 27.3 us  [on_device(): lax.all_to_all(up, 'kz', 0, 0, tiled=True, axis_index_groups=core_groups)]
    all_to_all x1, blocking collectives: 11.2 us -> 10.1 us  [on_device(): messages = lax.all_to_all(message, 'kx', 0, 0, tiled=True)]
where the time goes in v3:
time: 93 us; the launch traced here: 92.8 us
  blocking collectives  79.2 us (85%)
  starting transfers between devices  7.68 us (8%)
  Pallas kernels  5.62 us (6%)
    all_to_all x1, blocking collectives, on_device(): lax.all_to_all(up, 'kz', 0, 0, tiled=True, axis_index_groups=core_groups)  27.3 us
    all_to_all x1, blocking collectives, on_device(): lax.all_to_all(payload, both, 0, 0, tiled=True, axis_index_groups=wave_gr...  21.2 us
    all_to_all x1, blocking collectives, on_device(): lax.all_to_all(ends, 'kz', 0, 0, tiled=True, axis_index_groups=core_groups)  20.5 us
    all_to_all x1, blocking collectives, on_device(): messages = lax.all_to_all(message, 'kx', 0, 0, tiled=True)  10.1 us
    ppermute x1, starting transfers between devices, on_device(): received = lax.ppermute(send, 'kz', pairs)  4.44 us
    ppermute x1, starting transfers between devices, on_device(): swapped = lax.ppermute(forcing, 'kz', pairs)  3.24 us
    pallas_call x2, Pallas kernels, points(): pl.pallas_call(functools.partial(points_kernel, other), in_specs=[vmem] *...  2.53 us
    pallas_call x1, Pallas kernels, on_device(): pl.pallas_call(moments_kernel, in_specs=[vmem, hbm, vmem], out_specs=[vme...  1.96 us
  transfers between devices with their start and end apart: 2, of which 1 were waited for; matrix products, arithmetic and copies ran while one was open for 0% of the time, Pallas kernels for 2%

profile of v3, /device:TPU:1, one launch (start us, length us, event | category | flops | bytes accessed | tf_op | source)
XLA Modules:
  0.0 92.8 jit_solution(8295622969789933804)
XLA Ops:
  0.0 3.2 %collective-permute-start = (f32[6,4,128,256]{3,2,1,0:T(8,128)}, f32[6,4,128,256]{3,2,1,0:T(8,128)S(1)}, u32[]{:S(2)}, u32[]{:S(2)}) collective-permute-start(f32[6,4,128,256]{3,2,1,0:T(8,128)} %x_ref.5), channel_id=1, source_target_pairs={{0,1},{1,0},{2,3},{3,2},{4,5},{5,4},{6,7},{7,6},{8,9},{9,8},{10,11... | collective-permute-start | bytes 9437192 | tf_op jit(solution)/shard_map/ppermute | solution.py:384
  3.2 0.7 shard_map.37
  4.0 21.2 %all_to_all.20.w_ref = f32[32,2,128]{2,1,0:T(2,128)S(1)} all-to-all(f32[32,2,128]{2,1,0:T(2,128)S(1)} %shard_map.37), channel_id=1, replica_groups={{0,1,18,19,36,37,54,55,72,73,90,91,108,109,126,127,130,131,144,145,166,..., dimensions={0} | all-to-all | bytes 65536 | tf_op jit(solution)/shard_map/all_to_all | solution.py:398
  25.2 0.0 collective-permute-done.r_ref
  25.2 2.0 %shard_map.38 = (f32[16,12,8,128]{3,2,1,0:T(8,128)S(1)}, f32[16,4,8,128]{3,2,1,0:T(8,128)S(1)}, f32[128,128]{1,0:T(8,128)S(1)}, f32[128,128]{1,0:T(8,128)S(1)}, f32[128,128]{1,0:T(8,128)S(1)}) custom-call(f32[32,2,128]{2,1,0:T(2,128)S(1)} %all_to_all.20.w_ref, f32[6,4,128,256]{3,2,1,0:T(8,128)} %x_ref.5, f32[6,4,128,256]{3,2,1,0:T(8,128)S(1)} %collective-permute-done.r_ref), custom_call_target="tpu_custom_call" | custom-call | tf_op jit(solution)/shard_map/pallas_call | solution.py:399
  27.2 27.3 %all_to_all.21.m_ref = f32[16,12,8,128]{3,2,1,0:T(8,128)S(1)} all-to-all(f32[16,12,8,128]{3,2,1,0:T(8,128)S(1)} %get-tuple-element.12), channel_id=1, replica_groups={{0,2,4,6,8,10,12,14,16,18,20,22,24,26,28,30},{1,3,5,7,9,11,13,15,17,19,..., dimensions={0} | all-to-all | bytes 1572864 | tf_op jit(solution)/shard_map/all_to_all | solution.py:410
  54.5 0.0 copy-start
  54.5 0.1 shard_map.39
  54.7 10.1 %all_to_all.22.g_ref = f32[8,12,8,128]{3,2,1,0:T(8,128)S(1)} all-to-all(f32[8,12,8,128]{3,2,1,0:T(8,128)S(1)} %shard_map.39), channel_id=1, replica_groups=mesh['kx'=8,'kz'=32] {'kx'}, dimensions={0} | all-to-all | bytes 786432 | tf_op jit(solution)/shard_map/all_to_all | solution.py:412
  64.8 0.2 shard_map.40
  65.0 20.5 %all_to_all.23.b_ref = f32[16,8,8,128]{3,2,1,0:T(8,128)S(1)} all-to-all(f32[16,8,8,128]{3,2,1,0:T(8,128)S(1)} %shard_map.40), channel_id=1, replica_groups={{0,2,4,6,8,10,12,14,16,18,20,22,24,26,28,30},{1,3,5,7,9,11,13,15,17,19,..., dimensions={0} | all-to-all | bytes 1048576 | tf_op jit(solution)/shard_map/all_to_all | solution.py:414
  85.4 0.1 shard_map.41
  85.5 4.4 %collective-permute-start.1 = (f32[16,8,8,128]{3,2,1,0:T(8,128)S(1)}, f32[16,8,8,128]{3,2,1,0:T(8,128)S(1)}, u32[]{:S(2)}, u32[]{:S(2)}) collective-permute-start(f32[16,8,8,128]{3,2,1,0:T(8,128)S(1)} %get-tuple-element.16), channel_id=1, source_target_pairs={{0,1},{1,0},{2,3},{3,2},{4,5},{5,4},{6,7},{7,6},{8,9},{9,8},{10,11... | collective-permute-start | bytes 1572872 | tf_op jit(solution)/shard_map/ppermute | solution.py:416
  90.0 0.0 copy-done
  90.0 1.3 %shard_map.42.refs_0_ = f32[6,4,128,256]{3,2,1,0:T(8,128)} custom-call(f32[6,4,128,256]{3,2,1,0:T(8,128)S(1)} %copy-done, f32[16,8,8,128]{3,2,1,0:T(8,128)S(1)} %get-tuple-element.18.ends, f32[128,128]{1,0:T(8,128)S(1)} %get-tuple-element.13.q_ref), custom_call_target="tpu_custom_call" | custom-call | flops 8388608 | bytes 4194304 | tf_op jit(solution)/shard_map/pallas_call | solution.py:419
  91.2 0.3 collective-permute-done.1.ends
  91.5 1.3 %shard_map.43 = f32[6,4,128,256]{3,2,1,0:T(8,128)} custom-call(f32[6,4,128,256]{3,2,1,0:T(8,128)S(1)} %copy-done, f32[16,8,8,128]{3,2,1,0:T(8,128)S(1)} %collective-permute-done.1.ends, f32[128,128]{1,0:T(8,128)S(1)} %get-tuple-element.17.q_ref, f32[6,4,128,256]{3,2,1,0:T(8,128)} %shard_map.42.refs_0_), custom_call_target="tpu_custom_call", output_to_operand_aliasing={{}: (3, {})} | custom-call | flops 8388608 | bytes 4194304 | tf_op jit(solution)/shard_map/pallas_call | solution.py:419
Async XLA Ops:
  0.0 25.2 %collective-permute-start = (f32[6,4,128,256]{3,2,1,0:T(8,128)}, f32[6,4,128,256]{3,2,1,0:T(8,128)S(1)}, u32[]{:S(2)}, u32[]{:S(2)}) collective-permute-start(f32[6,4,128,256]{3,2,1,0:T(8,128)} %x_ref.5), channel_id=1, source_target_pairs={{0,1},{1,0},{2,3},{3,2},{4,5},{5,4},{6,7},{7,6},{8,9},{9,8},{10,11... | collective-permute-start | bytes 9437192 | tf_op jit(solution)/shard_map/ppermute | solution.py:384
  54.5 35.4 %copy-start = (f32[6,4,128,256]{3,2,1,0:T(8,128)S(1)}, f32[6,4,128,256]{3,2,1,0:T(8,128)}, u32[]{:S(2)}) copy-start(f32[6,4,128,256]{3,2,1,0:T(8,128)} %x_ref.5) | copy-start | bytes 9437188
  85.5 6.0 %collective-permute-start.1 = (f32[16,8,8,128]{3,2,1,0:T(8,128)S(1)}, f32[16,8,8,128]{3,2,1,0:T(8,128)S(1)}, u32[]{:S(2)}, u32[]{:S(2)}) collective-permute-start(f32[16,8,8,128]{3,2,1,0:T(8,128)S(1)} %get-tuple-element.16), channel_id=1, source_target_pairs={{0,1},{1,0},{2,3},{3,2},{4,5},{5,4},{6,7},{7,6},{8,9},{9,8},{10,11... | collective-permute-start | bytes 1572872 | tf_op jit(solution)/shard_map/ppermute | solution.py:416

commit v4 on v3

--- a/solution.py
+++ b/solution.py
@@ -17,6 +17,8 @@
 PTS = 6
 BLK = 12
 GRP = 16
+CHIPS = 128
+NUM = 12
 F32 = jnp.float32
 
 
@@ -76,7 +78,7 @@
         o_ref[j] = rows
 
 
-def moments_kernel(w_ref, x_ref, r_ref, up_ref, mid_ref, q_ref, qo_ref, ratio_ref, x_own, sems):
+def moments_kernel(w_ref, x_ref, r_ref, up_ref, mid_ref, q_ref, qo_ref, ratio_ref, x_own, stage, sems):
     core, _, _ = position()
     ty, tx = wave_group()
     chunks = sems.shape[0]
@@ -126,6 +128,9 @@
             pq = chain(H2 * q, BLK)
             ratio = ps[PTS] / ps[BLK]
             ratio_ref[rows, :] = ratio
+            def put(n, value):
+                stage[pl.ds(8 * NUM * i + n, 8, stride=NUM), :] = KAPPA * value
+
             for c in range(4):
                 f = [first(m, c, rows) for m in range(PTS)] + [second(m, c, rows) for m in range(PTS)]
                 own = ps[BLK] * f[0]
@@ -137,8 +142,8 @@
                     own = own + to_own
                     nxt = nxt + to_nxt
                     mid = mid + (to_nxt if m <= PTS else to_own)
-                up_ref[i, c] = KAPPA * own
-                up_ref[i, 4 + c] = KAPPA * nxt
+                put(c, own)
+                put(4 + c, nxt)
                 mid_ref[i, c] = ratio * (KAPPA * mid)
                 if c < 2:
                     own = pq[BLK] * f[0]
@@ -147,8 +152,8 @@
                         own = own + pq[BLK - m] * f[m]
                     for m in range(2, BLK):
                         nxt = nxt + pq[m] * f[m]
-                    up_ref[i, 8 + c] = KAPPA * own
-                    up_ref[i, 10 + c] = KAPPA * nxt
+                    put(8 + c, own)
+                    put(10 + c, nxt)
 
     for g in range(chunks):
         copy(g, 0).wait()
@@ -161,61 +166,28 @@
         def _():
             tiles(g, lambda m, c, rows: r_ref[m, c, rows, 128:], lambda m, c, rows: x_own[m, c, rows, :])
 
-
-def sources(m_ref, own, nxt):
-    return (
-        [m_ref[0, own]]
-        + [m_ref[d, own] + m_ref[d - 1, nxt] for d in range(1, GRP)]
-        + [m_ref[GRP - 1, nxt]]
-    )
-
-
-def group_kernel(m_ref, q_ref, o_ref):
+    @pl.loop(0, 64, unroll=4)
+    def _(i):
+        for k in range(3):
+            value = stage[pl.ds(pl.multiple_of(24 * i + 8 * k, 8), 8), :]
+            for half in range(2):
+                j, a = divmod(2 * k + half, 3)
+                up_ref[2 * i + j, a] = value[4 * half : 4 * half + 4, :]
+
+
+def solve_kernel(m_ref, q_ref, o_ref):
     _, group, chip = position()
-    q = q_ref[pl.ds(pl.multiple_of(8 * chip, 8), 8), :]
-    rho = jnp.exp(-BLK * angle(H2 * (q + SHIFT)))
-    res = [None] * 12
-    for c in range(4):
-        t = sources(m_ref, c, 4 + c)
-        right = t[0]
-        for d in range(1, GRP + 1):
-            right = rho * right + t[d]
-        left = t[GRP]
-        for d in range(GRP - 1, -1, -1):
-            left = rho * left + t[d]
-        res[c] = right
-        res[4 + c] = left
-    tq = angle(H2 * q)
-    end = jnp.exp(-N * tq)
-    inv = 1.0 / jnp.where(q > 0.0, 1.0 - end * end, 1.0)
-    sq = [sources(m_ref, 8 + c, 10 + c) for c in range(2)]
-    for c in range(2):
-        res[8 + c] = jnp.zeros_like(q)
-        res[10 + c] = jnp.zeros_like(q)
-    for d in range(GRP + 1):
-        place = (BLK * (GRP * group + d) + 1).astype(F32)
-        fall = jnp.exp(-place * tq)
-        rise = (jnp.exp((place - N) * tq) - end * fall) * inv
-        rise = jnp.where(q > 0.0, rise, place * (1.0 / N))
-        fall = fall - end * rise
-        for c in range(2):
-            res[8 + c] = res[8 + c] + fall * sq[c][d]
-            res[10 + c] = res[10 + c] + rise * sq[c][d]
-    for k in range(o_ref.shape[0]):
-        for n in range(12):
-            o_ref[k, n] = res[n]
-
-
-def solve_kernel(m_ref, g_ref, q_ref, o_ref):
-    _, group, chip = position()
-    groups = g_ref.shape[0]
-    q = q_ref[pl.ds(pl.multiple_of(8 * chip, 8), 8), :]
+    shape = (4, 128)
+    q = jnp.broadcast_to(q_ref[pl.ds(GRP * group + chip, 1), :], shape)
+    sub = lax.broadcasted_iota(jnp.int32, shape, 0)
     es = H2 * (q + SHIFT)
     eq = H2 * q
     ts = angle(es)
     tq = angle(eq)
     rho = jnp.exp(-BLK * ts)
-    rho_g = jnp.exp(-(BLK * GRP) * ts)
+    rho_seg = jnp.exp(-(BLK * GRP) * ts)
+    rho_q = jnp.exp(-BLK * tq)
+    rho_q_seg = jnp.exp(-(BLK * GRP) * tq)
     sinh_s = jnp.sqrt(es * (1.0 + 0.25 * es))
     sinh_q = jnp.sqrt(eq * (1.0 + 0.25 * eq))
     scale = 0.5 / (sinh_s * chain(es, BLK)[BLK])
@@ -232,60 +204,89 @@
     m_cross = (2.0 - eq) * csch_q - (2.0 - es) * csch_s
     inv_det = 1.0 / (m_same * m_same - m_cross * m_cross)
     inv_pq = 1.0 / chain(eq, BLK)[BLK]
-    gf = group.astype(F32)
-    near = jnp.exp(-(gf * (BLK * GRP) + 1.0) * ts)
-    far = jnp.exp(-(NY - BLK * GRP - gf * (BLK * GRP)) * ts)
-    first = jnp.exp(-ts)
-    for c in range(4):
-        at_hi = g_ref[0, c]
-        from_lo = jnp.zeros_like(q)
-        for k in range(groups):
-            if k:
-                at_hi = rho_g * at_hi + g_ref[k, c]
-            from_lo = jnp.where(k < group, rho_g * from_lo + g_ref[k, c], from_lo)
-        at_lo = g_ref[groups - 1, 4 + c]
-        from_hi = jnp.zeros_like(q)
-        for k in range(groups - 1, -1, -1):
-            if k < groups - 1:
-                at_lo = rho_g * at_lo + g_ref[k, 4 + c]
-            from_hi = jnp.where(k > group, rho_g * from_hi + g_ref[k, 4 + c], from_hi)
-        x_lo = scale * first * at_lo
-        x_hi = scale * at_hi
-        if c < 2:
-            y_lo = g_ref[0, 8 + c]
-            y_hi = g_ref[0, 10 + c]
-            for k in range(1, groups):
-                y_lo = y_lo + g_ref[k, 8 + c]
-                y_hi = y_hi + g_ref[k, 10 + c]
-            alpha = (end_s * x_hi - x_lo) * inv_s
-            beta = (end_s * x_lo - x_hi) * inv_s
-            phi_lo = 2.0 * sinh_s * (x_lo + end_s * beta)
-            phi_hi = 2.0 * sinh_s * (x_hi + end_s * alpha)
-            w_lo = (2.0 - es) * phi_lo - (2.0 - eq) * (y_lo * inv_pq)
-            w_hi = (2.0 - es) * phi_hi - (2.0 - eq) * (y_hi * inv_pq)
-            wall_lo = (m_same * w_lo - m_cross * w_hi) * inv_det - x_lo
-            wall_hi = (m_same * w_hi - m_cross * w_lo) * inv_det - x_hi
-        else:
-            wall_lo = -x_lo
-            wall_hi = -x_hi
-        alpha = (wall_lo - end_s * wall_hi) * inv_s
-        beta = (wall_hi - end_s * wall_lo) * inv_s
-        t = [scale * v for v in sources(m_ref, c, 4 + c)]
-        back = scale * from_hi + beta * far
-        falls = [None] * (GRP + 1)
-        falls[GRP] = back
-        for d in range(GRP - 1, -1, -1):
-            back = rho * (back + t[d + 1])
-            falls[d] = back
-        ahead = scale * from_lo + alpha * near + t[0]
-        for d in range(GRP + 1):
+
+    segments = CHIPS // GRP
+    ends, heads, falls, rises, firsts = [], [], [], [], []
+    for k in range(segments):
+        t = []
+        for d in range(GRP * k, GRP * (k + 1)):
+            value = m_ref[d, 0]
+            t.append(value + m_ref[d - 1, 1] if d else value)
+        ahead = [t[0]]
+        for v in t[1:]:
+            ahead.append(rho * ahead[-1] + v)
+        ends.append(ahead[-1])
+        back = t[-1]
+        o_ref[GRP * k + GRP - 1, 0:4, :] = scale * ahead[-1]
+        for i in range(GRP - 2, -1, -1):
+            o_ref[GRP * k + i, 0:4, :] = scale * (ahead[i] + rho * back)
+            back = t[i] + rho * back
+        heads.append(back)
+        w = [m_ref[d, 2] for d in range(GRP * k, GRP * (k + 1))]
+        rise = w[0]
+        first = (GRP * k) * w[0]
+        for i in range(1, GRP):
+            rise = rho_q * rise + w[i]
+            first = first + (GRP * k + i) * w[i]
+        fall = w[-1]
+        for i in range(GRP - 2, -1, -1):
+            fall = w[i] + rho_q * fall
+        falls.append(fall)
+        rises.append(rise)
+        firsts.append(first)
+
+    last = m_ref[CHIPS - 1, 1]
+    from_lo = [jnp.zeros(shape, F32)]
+    for k in range(segments):
+        from_lo.append(ends[k] + rho_seg * from_lo[-1])
+    at_hi = rho * from_lo[segments] + last
+    from_hi = [None] * segments
+    value = last
+    for k in range(segments - 1, -1, -1):
+        from_hi[k] = value
+        value = heads[k] + rho_seg * value
+    at_lo = value
+    fall, rise, first = falls[-1], rises[0], firsts[0]
+    for k in range(1, segments):
+        fall = falls[segments - 1 - k] + rho_q_seg * fall
+        rise = rises[k] + rho_q_seg * rise
+        first = first + firsts[k]
+
+    place = jnp.where(sub < 2, 1.0, BLK + 1.0)
+    lower = jnp.exp(-place * tq) * fall
+    upper = jnp.where(sub < 2, rho_q, 1.0) * rise
+    y_hi = jnp.where(positive, (upper - end_q * lower) * inv_q, (BLK * first + place * fall) * (1.0 / N))
+    y_lo = lower - end_q * y_hi
+
+    def both(value):
+        return jnp.concatenate([value[0:2] + value[2:4], jnp.zeros((2, 128), F32)], axis=0)
+
+    x_lo = scale * jnp.exp(-ts) * at_lo
+    x_hi = scale * at_hi
+    alpha = (end_s * x_hi - x_lo) * inv_s
+    beta = (end_s * x_lo - x_hi) * inv_s
+    phi_lo = 2.0 * sinh_s * (x_lo + end_s * beta)
+    phi_hi = 2.0 * sinh_s * (x_hi + end_s * alpha)
+    w_lo = (2.0 - es) * phi_lo - (2.0 - eq) * (both(y_lo) * inv_pq)
+    w_hi = (2.0 - es) * phi_hi - (2.0 - eq) * (both(y_hi) * inv_pq)
+    wall_lo = jnp.where(sub < 2, (m_same * w_lo - m_cross * w_hi) * inv_det, 0.0) - x_lo
+    wall_hi = jnp.where(sub < 2, (m_same * w_hi - m_cross * w_lo) * inv_det, 0.0) - x_hi
+    alpha = (wall_lo - end_s * wall_hi) * inv_s
+    beta = (wall_hi - end_s * wall_lo) * inv_s
+
+    power = [None, rho]
+    for _ in range(GRP - 1):
+        power.append(power[-1] * rho)
+    for k in range(segments):
+        up = scale * from_lo[k] + alpha * jnp.exp((BLK - 1.0 - BLK * GRP * k) * ts)
+        down = scale * from_hi[k] + beta * jnp.exp((BLK * GRP * (k + 1.0) - NY) * ts)
+        for i in range(GRP):
+            d = GRP * k + i
+            value = o_ref[d, 0:4, :] + power[i + 1] * up + power[GRP - i] * down
+            o_ref[d, 0:4, :] = value
             if d:
-                ahead = rho * ahead + t[d]
-            value = ahead + falls[d]
-            if d < GRP:
-                o_ref[d, c] = value
-            if d:
-                o_ref[d - 1, 4 + c] = value
+                o_ref[d - 1, 4:8, :] = value
+    o_ref[CHIPS - 1, 4:8, :] = x_hi + alpha * end_s + beta
 
 
 def middle_kernel(b_ref, mid_ref, ratio_ref, own_ref, send_ref):
@@ -296,8 +297,8 @@
         def _(i):
             ratio = ratio_ref[pl.ds(pl.multiple_of(8 * i, 8), 8), :]
             for c in range(4):
-                a = b_ref[i, c]
-                b = b_ref[i, 4 + c]
+                a = b_ref[pl.ds(64 * i + c, 8, stride=8), :]
+                b = b_ref[pl.ds(64 * i + 4 + c, 8, stride=8), :]
                 x = ratio * (a + b) + mid_ref[i, c]
                 lower[i, c] = a
                 lower[i, 4 + c] = x
@@ -373,7 +374,7 @@
     wave_groups = [
         [32 * (j // 4) + wave_member(j, ty, tx) for j in range(32)] for ty in range(4) for tx in range(2)
     ]
-    core_groups = [[2 * k + c for k in range(GRP)] for c in range(2)]
+    core_groups = [[2 * k + c for k in range(CHIPS)] for c in range(2)]
     pairs = [(i, i ^ 1) for i in range(32)]
 
     vmem = pl.BlockSpec(memory_space=pltpu.VMEM)
@@ -402,16 +403,19 @@
         out_specs=[vmem] * 5,
         out_shape=[
             pltpu.VMEM(shape, F32)
-            for shape in ((GRP, 12, 8, 128), (GRP, 4, 8, 128), (128, 128), (128, 128), (128, 128))
+            for shape in ((CHIPS, 3, 4, 128), (GRP, 4, 8, 128), (128, 128), (128, 128), (128, 128))
         ],
-        scratch_shapes=[pltpu.VMEM(half_shape, F32), pltpu.SemaphoreType.DMA((4,))],
+        scratch_shapes=[
+            pltpu.VMEM(half_shape, F32),
+            pltpu.VMEM((NUM * CHIPS, 128), F32),
+            pltpu.SemaphoreType.DMA((4,)),
+        ],
         compiler_params=params,
     )(in_vmem(waves), pltpu.with_memory_space_constraint(forcing, pltpu.HBM), in_vmem(swapped))
-    blocks = lax.all_to_all(up, "kz", 0, 0, tiled=True, axis_index_groups=core_groups)
-    (message,) = local_call(group_kernel, (blocks, q_own), ((8, 12, 8, 128),))
-    messages = lax.all_to_all(message, "kx", 0, 0, tiled=True)
-    (ends,) = local_call(solve_kernel, (blocks, messages, q_own), ((GRP, 8, 8, 128),))
-    ends = lax.all_to_all(ends, "kz", 0, 0, tiled=True, axis_index_groups=core_groups)
+    blocks = lax.all_to_all(up, both, 0, 0, tiled=True, axis_index_groups=core_groups)
+    (ends,) = local_call(solve_kernel, (blocks, q_own), ((CHIPS, 8, 128),))
+    ends = lax.all_to_all(ends, both, 0, 0, tiled=True, axis_index_groups=core_groups)
+    ends = ends.reshape(8 * CHIPS, 128)
     own, send = local_call(middle_kernel, (ends, mid, ratio), ((GRP, 8, 8, 128),) * 2)
     received = lax.ppermute(send, "kz", pairs)
 

time: 93 us -> 88.4 us (0.951)
  blocking collectives: 79.2 us -> 75.1 us
    all_to_all x3 -> x2, blocking collectives: 57.9 us -> 53.9 us  [the longest x1 28.4 us: on_device(): lax.all_to_all(up, both, 0, 0, tiled=True, axis_index_groups=core_groups)]
where the time goes in v4:
time: 88.4 us; the launch traced here: 88.2 us
  blocking collectives  75.1 us (85%)
  starting transfers between devices  6.85 us (8%)
  Pallas kernels  5.9 us (7%)
    all_to_all x1, blocking collectives, on_device(): lax.all_to_all(up, both, 0, 0, tiled=True, axis_index_groups=core_groups)  28.4 us
    all_to_all x1, blocking collectives, on_device(): lax.all_to_all(ends, both, 0, 0, tiled=True, axis_index_groups=core_groups)  25.5 us
    all_to_all x1, blocking collectives, on_device(): lax.all_to_all(payload, both, 0, 0, tiled=True, axis_index_groups=wave_gr...  21.2 us
    ppermute x1, starting transfers between devices, on_device(): received = lax.ppermute(send, 'kz', pairs)  3.61 us
    ppermute x1, starting transfers between devices, on_device(): swapped = lax.ppermute(forcing, 'kz', pairs)  3.24 us
    pallas_call x2, Pallas kernels, points(): pl.pallas_call(functools.partial(points_kernel, other), in_specs=[vmem] *...  2.53 us
    pallas_call x1, Pallas kernels, on_device(): pl.pallas_call(moments_kernel, in_specs=[vmem, hbm, vmem], out_specs=[vme...  2.12 us
  transfers between devices with their start and end apart: 2, of which 1 were waited for; matrix products, arithmetic and copies ran while one was open for 0% of the time, Pallas kernels for 2%

profile of v4, /device:TPU:1, one launch (start us, length us, event | category | flops | bytes accessed | tf_op | source)
XLA Modules:
  0.0 88.2 jit_solution(1072832916806000742)
XLA Ops:
  0.0 3.2 %collective-permute-start = (f32[6,4,128,256]{3,2,1,0:T(8,128)}, f32[6,4,128,256]{3,2,1,0:T(8,128)S(1)}, u32[]{:S(2)}, u32[]{:S(2)}) collective-permute-start(f32[6,4,128,256]{3,2,1,0:T(8,128)} %x_ref.5), channel_id=1, source_target_pairs={{0,1},{1,0},{2,3},{3,2},{4,5},{5,4},{6,7},{7,6},{8,9},{9,8},{10,11... | collective-permute-start | bytes 9437192 | tf_op jit(solution)/shard_map/ppermute | solution.py:385
  3.2 0.7 shard_map.37
  4.0 21.2 %all_to_all.15.w_ref = f32[32,2,128]{2,1,0:T(2,128)S(1)} all-to-all(f32[32,2,128]{2,1,0:T(2,128)S(1)} %shard_map.37), channel_id=1, replica_groups={{0,1,18,19,36,37,54,55,72,73,90,91,108,109,126,127,130,131,144,145,166,..., dimensions={0} | all-to-all | bytes 65536 | tf_op jit(solution)/shard_map/all_to_all | solution.py:399
  25.2 0.0 collective-permute-done.r_ref
  25.2 2.1 %shard_map.38 = (f32[128,3,4,128]{3,2,1,0:T(4,128)S(1)}, f32[16,4,8,128]{3,2,1,0:T(8,128)S(1)}, f32[128,128]{1,0:T(8,128)S(1)}, f32[128,128]{1,0:T(8,128)S(1)}, f32[128,128]{1,0:T(8,128)S(1)}) custom-call(f32[32,2,128]{2,1,0:T(2,128)S(1)} %all_to_all.15.w_ref, f32[6,4,128,256]{3,2,1,0:T(8,128)} %x_ref.5, f32[6,4,128,256]{3,2,1,0:T(8,128)S(1)} %collective-permute-done.r_ref), custom_call_target="tpu_custom_call" | custom-call | tf_op jit(solution)/shard_map/pallas_call | solution.py:400
  27.3 0.0 copy-start
  27.3 28.4 %all_to_all.16.m_ref = f32[128,3,4,128]{3,2,1,0:T(4,128)S(1)} all-to-all(f32[128,3,4,128]{3,2,1,0:T(4,128)S(1)} %get-tuple-element.12), channel_id=1, replica_groups={{0,2,4,6,8,10,12,14,16,18,20,22,24,26,28,30,32,34,36,38,40,42,44,46,48,..., dimensions={0} | all-to-all | bytes 1572864 | tf_op jit(solution)/shard_map/all_to_all | solution.py:415
  55.7 0.4 shard_map.39
  56.1 25.5 %all_to_all.17 = f32[128,8,128]{2,1,0:T(8,128)S(1)} all-to-all(f32[128,8,128]{2,1,0:T(8,128)S(1)} %shard_map.39), channel_id=1, replica_groups={{0,2,4,6,8,10,12,14,16,18,20,22,24,26,28,30,32,34,36,38,40,42,44,46,48,..., dimensions={0} | all-to-all | bytes 1048576 | tf_op jit(solution)/shard_map/all_to_all | solution.py:417
  81.6 0.2 shard_map.40
  81.8 3.6 %collective-permute-start.1 = (f32[16,8,8,128]{3,2,1,0:T(8,128)S(1)}, f32[16,8,8,128]{3,2,1,0:T(8,128)S(1)}, u32[]{:S(2)}, u32[]{:S(2)}) collective-permute-start(f32[16,8,8,128]{3,2,1,0:T(8,128)S(1)} %get-tuple-element.16), channel_id=1, source_target_pairs={{0,1},{1,0},{2,3},{3,2},{4,5},{5,4},{6,7},{7,6},{8,9},{9,8},{10,11... | collective-permute-start | bytes 1572872 | tf_op jit(solution)/shard_map/ppermute | solution.py:420
  85.4 0.0 copy-done
  85.4 1.3 %shard_map.41.refs_0_ = f32[6,4,128,256]{3,2,1,0:T(8,128)} custom-call(f32[6,4,128,256]{3,2,1,0:T(8,128)S(1)} %copy-done, f32[16,8,8,128]{3,2,1,0:T(8,128)S(1)} %get-tuple-element.18.ends, f32[128,128]{1,0:T(8,128)S(1)} %get-tuple-element.13.q_ref), custom_call_target="tpu_custom_call" | custom-call | flops 8388608 | bytes 4194304 | tf_op jit(solution)/shard_map/pallas_call | solution.py:423
  86.7 0.3 collective-permute-done.1.ends
  86.9 1.3 %shard_map.42 = f32[6,4,128,256]{3,2,1,0:T(8,128)} custom-call(f32[6,4,128,256]{3,2,1,0:T(8,128)S(1)} %copy-done, f32[16,8,8,128]{3,2,1,0:T(8,128)S(1)} %collective-permute-done.1.ends, f32[128,128]{1,0:T(8,128)S(1)} %get-tuple-element.17.q_ref, f32[6,4,128,256]{3,2,1,0:T(8,128)} %shard_map.41.refs_0_), custom_call_target="tpu_custom_call", output_to_operand_aliasing={{}: (3, {})} | custom-call | flops 8388608 | bytes 4194304 | tf_op jit(solution)/shard_map/pallas_call | solution.py:423
Async XLA Ops:
  0.0 25.2 %collective-permute-start = (f32[6,4,128,256]{3,2,1,0:T(8,128)}, f32[6,4,128,256]{3,2,1,0:T(8,128)S(1)}, u32[]{:S(2)}, u32[]{:S(2)}) collective-permute-start(f32[6,4,128,256]{3,2,1,0:T(8,128)} %x_ref.5), channel_id=1, source_target_pairs={{0,1},{1,0},{2,3},{3,2},{4,5},{5,4},{6,7},{7,6},{8,9},{9,8},{10,11... | collective-permute-start | bytes 9437192 | tf_op jit(solution)/shard_map/ppermute | solution.py:385
  27.3 58.1 %copy-start = (f32[6,4,128,256]{3,2,1,0:T(8,128)S(1)}, f32[6,4,128,256]{3,2,1,0:T(8,128)}, u32[]{:S(2)}) copy-start(f32[6,4,128,256]{3,2,1,0:T(8,128)} %x_ref.5) | copy-start | bytes 9437188
  81.8 5.1 %collective-permute-start.1 = (f32[16,8,8,128]{3,2,1,0:T(8,128)S(1)}, f32[16,8,8,128]{3,2,1,0:T(8,128)S(1)}, u32[]{:S(2)}, u32[]{:S(2)}) collective-permute-start(f32[16,8,8,128]{3,2,1,0:T(8,128)S(1)} %get-tuple-element.16), channel_id=1, source_target_pairs={{0,1},{1,0},{2,3},{3,2},{4,5},{5,4},{6,7},{7,6},{8,9},{9,8},{10,11... | collective-permute-start | bytes 1572872 | tf_op jit(solution)/shard_map/ppermute | solution.py:420

commit v5 on v4

--- a/solution.py
+++ b/solution.py
@@ -78,7 +78,7 @@
         o_ref[j] = rows
 
 
-def moments_kernel(w_ref, x_ref, r_ref, up_ref, mid_ref, q_ref, qo_ref, ratio_ref, x_own, stage, sems):
+def moments_kernel(w_ref, x_ref, r_ref, turn_ref, up_ref, mid_ref, q_ref, qo_ref, ratio_ref, x_own, stage, sems):
     core, _, _ = position()
     ty, tx = wave_group()
     chunks = sems.shape[0]
@@ -397,9 +397,11 @@
         compiler_params=params,
     )(*[pltpu.with_memory_space_constraint(v, pltpu.HBM) for v in (kx_wave, kz_wave)])
     waves = lax.all_to_all(payload, both, 0, 0, tiled=True, axis_index_groups=wave_groups)
+    turn = lax.ppermute(waves, "kz", [(i, i ^ 2) for i in range(0, 32, 2)])
+
     up, mid, q_own, q_oth, ratio = pl.pallas_call(
         moments_kernel,
-        in_specs=[vmem, hbm, vmem],
+        in_specs=[vmem, hbm, vmem, vmem],
         out_specs=[vmem] * 5,
         out_shape=[
             pltpu.VMEM(shape, F32)
@@ -411,7 +413,7 @@
             pltpu.SemaphoreType.DMA((4,)),
         ],
         compiler_params=params,
-    )(in_vmem(waves), pltpu.with_memory_space_constraint(forcing, pltpu.HBM), in_vmem(swapped))
+    )(in_vmem(waves), pltpu.with_memory_space_constraint(forcing, pltpu.HBM), in_vmem(swapped), in_vmem(turn))
     blocks = lax.all_to_all(up, both, 0, 0, tiled=True, axis_index_groups=core_groups)
     (ends,) = local_call(solve_kernel, (blocks, q_own), ((CHIPS, 8, 128),))
     ends = lax.all_to_all(ends, both, 0, 0, tiled=True, axis_index_groups=core_groups)

time: 88.4 us -> 85.8 us (0.971)
  blocking collectives: 75.1 us -> 65.4 us
  starting transfers between devices: 6.85 us -> 13.8 us
    ppermute x1, starting transfers between devices: 3.61 us -> 9.95 us  [on_device(): received = lax.ppermute(send, 'kz', pairs)]
    all_to_all x1, blocking collectives: 28.4 us -> 22.7 us  [on_device(): lax.all_to_all(up, both, 0, 0, tiled=True, axis_index_groups=core_groups)]
    all_to_all x1, blocking collectives: 25.5 us -> 21.5 us  [on_device(): lax.all_to_all(ends, both, 0, 0, tiled=True, axis_index_groups=core_groups)]
  transfers between devices with their start and end apart: 2 -> 3, of which waited for: 1 -> 1; matrix products, arithmetic and copies ran while one was open for 0% -> 0% of each run, Pallas kernels for 2% -> 2%
where the time goes in v5:
time: 85.8 us; the launch traced here: 85.6 us
  blocking collectives  65.4 us (76%)
  starting transfers between devices  13.8 us (16%)
  Pallas kernels  5.95 us (7%)
    all_to_all x1, blocking collectives, on_device(): lax.all_to_all(up, both, 0, 0, tiled=True, axis_index_groups=core_groups)  22.7 us
    all_to_all x1, blocking collectives, on_device(): lax.all_to_all(ends, both, 0, 0, tiled=True, axis_index_groups=core_groups)  21.5 us
    all_to_all x1, blocking collectives, on_device(): lax.all_to_all(payload, both, 0, 0, tiled=True, axis_index_groups=wave_gr...  21.2 us
    ppermute x1, starting transfers between devices, on_device(): received = lax.ppermute(send, 'kz', pairs)  9.95 us
    ppermute x1, starting transfers between devices, on_device(): swapped = lax.ppermute(forcing, 'kz', pairs)  3.24 us
    pallas_call x2, Pallas kernels, points(): pl.pallas_call(functools.partial(points_kernel, other), in_specs=[vmem] *...  2.53 us
    pallas_call x1, Pallas kernels, on_device(): pl.pallas_call(moments_kernel, in_specs=[vmem, hbm, vmem, vmem], out_spec...  2.16 us
  transfers between devices with their start and end apart: 3, of which 1 were waited for; matrix products, arithmetic and copies ran while one was open for 0% of the time, Pallas kernels for 2%

profile of v5, /device:TPU:1, one launch (start us, length us, event | category | flops | bytes accessed | tf_op | source)
XLA Modules:
  0.0 85.6 jit_solution(8811210581606895929)
XLA Ops:
  0.0 3.2 %collective-permute-start = (f32[6,4,128,256]{3,2,1,0:T(8,128)}, f32[6,4,128,256]{3,2,1,0:T(8,128)S(1)}, u32[]{:S(2)}, u32[]{:S(2)}) collective-permute-start(f32[6,4,128,256]{3,2,1,0:T(8,128)} %x_ref.5), channel_id=1, source_target_pairs={{0,1},{1,0},{2,3},{3,2},{4,5},{5,4},{6,7},{7,6},{8,9},{9,8},{10,11... | collective-permute-start | bytes 9437192 | tf_op jit(solution)/shard_map/ppermute | solution.py:385
  3.2 0.7 shard_map.37
  4.0 21.2 %all_to_all.15.w_ref = f32[32,2,128]{2,1,0:T(2,128)S(1)} all-to-all(f32[32,2,128]{2,1,0:T(2,128)S(1)} %shard_map.37), channel_id=1, replica_groups={{0,1,18,19,36,37,54,55,72,73,90,91,108,109,126,127,130,131,144,145,166,..., dimensions={0} | all-to-all | bytes 65536 | tf_op jit(solution)/shard_map/all_to_all | solution.py:399
  25.2 0.7 collective-permute-start.1
  25.9 0.0 collective-permute-done.1.turn_ref
  25.9 0.0 collective-permute-done.r_ref
  25.9 2.2 %shard_map.38 = (f32[128,3,4,128]{3,2,1,0:T(4,128)S(1)}, f32[16,4,8,128]{3,2,1,0:T(8,128)S(1)}, f32[128,128]{1,0:T(8,128)S(1)}, f32[128,128]{1,0:T(8,128)S(1)}, f32[128,128]{1,0:T(8,128)S(1)}) custom-call(f32[32,2,128]{2,1,0:T(2,128)S(1)} %all_to_all.15.w_ref, f32[6,4,128,256]{3,2,1,0:T(8,128)} %x_ref.5, f32[6,4,128,256]{3,2,1,0:T(8,128)S(1)} %collective-permute-done.r_ref, ...), custom_call_target="tpu_custom_call" | custom-call | tf_op jit(solution)/shard_map/pallas_call | solution.py:402
  28.1 0.0 copy-start
  28.1 22.7 %all_to_all.16.m_ref = f32[128,3,4,128]{3,2,1,0:T(4,128)S(1)} all-to-all(f32[128,3,4,128]{3,2,1,0:T(4,128)S(1)} %get-tuple-element.12), channel_id=1, replica_groups={{0,2,4,6,8,10,12,14,16,18,20,22,24,26,28,30,32,34,36,38,40,42,44,46,48,..., dimensions={0} | all-to-all | bytes 1572864 | tf_op jit(solution)/shard_map/all_to_all | solution.py:417
  50.8 0.4 shard_map.39
  51.2 21.5 %all_to_all.17 = f32[128,8,128]{2,1,0:T(8,128)S(1)} all-to-all(f32[128,8,128]{2,1,0:T(8,128)S(1)} %shard_map.39), channel_id=1, replica_groups={{0,2,4,6,8,10,12,14,16,18,20,22,24,26,28,30,32,34,36,38,40,42,44,46,48,..., dimensions={0} | all-to-all | bytes 1048576 | tf_op jit(solution)/shard_map/all_to_all | solution.py:419
  72.7 0.2 shard_map.40
  72.8 10.0 %collective-permute-start.2 = (f32[16,8,8,128]{3,2,1,0:T(8,128)S(1)}, f32[16,8,8,128]{3,2,1,0:T(8,128)S(1)}, u32[]{:S(2)}, u32[]{:S(2)}) collective-permute-start(f32[16,8,8,128]{3,2,1,0:T(8,128)S(1)} %get-tuple-element.16), channel_id=1, source_target_pairs={{0,1},{1,0},{2,3},{3,2},{4,5},{5,4},{6,7},{7,6},{8,9},{9,8},{10,11... | collective-permute-start | bytes 1572872 | tf_op jit(solution)/shard_map/ppermute | solution.py:422
  82.8 0.0 copy-done
  82.8 1.3 %shard_map.41.refs_0_ = f32[6,4,128,256]{3,2,1,0:T(8,128)} custom-call(f32[6,4,128,256]{3,2,1,0:T(8,128)S(1)} %copy-done, f32[16,8,8,128]{3,2,1,0:T(8,128)S(1)} %get-tuple-element.18.ends, f32[128,128]{1,0:T(8,128)S(1)} %get-tuple-element.13.q_ref), custom_call_target="tpu_custom_call" | custom-call | flops 8388608 | bytes 4194304 | tf_op jit(solution)/shard_map/pallas_call | solution.py:425
  84.0 0.3 collective-permute-done.2.ends
  84.3 1.3 %shard_map.42 = f32[6,4,128,256]{3,2,1,0:T(8,128)} custom-call(f32[6,4,128,256]{3,2,1,0:T(8,128)S(1)} %copy-done, f32[16,8,8,128]{3,2,1,0:T(8,128)S(1)} %collective-permute-done.2.ends, f32[128,128]{1,0:T(8,128)S(1)} %get-tuple-element.17.q_ref, f32[6,4,128,256]{3,2,1,0:T(8,128)} %shard_map.41.refs_0_), custom_call_target="tpu_custom_call", output_to_operand_aliasing={{}: (3, {})} | custom-call | flops 8388608 | bytes 4194304 | tf_op jit(solution)/shard_map/pallas_call | solution.py:425
Async XLA Ops:
  0.0 25.9 %collective-permute-start = (f32[6,4,128,256]{3,2,1,0:T(8,128)}, f32[6,4,128,256]{3,2,1,0:T(8,128)S(1)}, u32[]{:S(2)}, u32[]{:S(2)}) collective-permute-start(f32[6,4,128,256]{3,2,1,0:T(8,128)} %x_ref.5), channel_id=1, source_target_pairs={{0,1},{1,0},{2,3},{3,2},{4,5},{5,4},{6,7},{7,6},{8,9},{9,8},{10,11... | collective-permute-start | bytes 9437192 | tf_op jit(solution)/shard_map/ppermute | solution.py:385
  25.2 0.7 collective-permute-start.1
  28.1 54.7 %copy-start = (f32[6,4,128,256]{3,2,1,0:T(8,128)S(1)}, f32[6,4,128,256]{3,2,1,0:T(8,128)}, u32[]{:S(2)}) copy-start(f32[6,4,128,256]{3,2,1,0:T(8,128)} %x_ref.5) | copy-start | bytes 9437188
  72.8 11.5 %collective-permute-start.2 = (f32[16,8,8,128]{3,2,1,0:T(8,128)S(1)}, f32[16,8,8,128]{3,2,1,0:T(8,128)S(1)}, u32[]{:S(2)}, u32[]{:S(2)}) collective-permute-start(f32[16,8,8,128]{3,2,1,0:T(8,128)S(1)} %get-tuple-element.16), channel_id=1, source_target_pairs={{0,1},{1,0},{2,3},{3,2},{4,5},{5,4},{6,7},{7,6},{8,9},{9,8},{10,11... | collective-permute-start | bytes 1572872 | tf_op jit(solution)/shard_map/ppermute | solution.py:422

commit v6 on v5

--- a/solution.py
+++ b/solution.py
@@ -32,12 +32,12 @@
     iz = lax.axis_index("kz")
     x_lo, y = lax.div(ix, 4), lax.rem(ix, 4)
     z, x_hi = lax.div(iz, 4), lax.rem(lax.div(iz, 2), 2)
-    return lax.rem(y - z + 8, 4), lax.rem(x_lo + x_hi + lax.div(z, 4), 2)
+    return lax.rem(y - z + 8, 4), lax.rem(x_lo + x_hi, 2)
 
 
 def wave_member(j, ty, tx):
     x_lo, y, b, core = j // 16, j // 4 % 4, j // 2 % 2, j % 2
-    return 4 * ((y - ty + 4) % 4 + 4 * b) + 2 * ((x_lo + tx + b) % 2) + core
+    return 4 * ((y - ty + 4) % 4 + 4 * b) + 2 * ((x_lo + tx) % 2) + core
 
 
 def chain(eps, n):

time: 85.8 us -> 84.9 us (0.990)
  no operation moved by 1% of the time
where the time goes in v6:
time: 84.9 us; the launch traced here: 84.7 us
  blocking collectives  64.7 us (76%)
  starting transfers between devices  13.7 us (16%)
  Pallas kernels  5.93 us (7%)
    all_to_all x1, blocking collectives, on_device(): lax.all_to_all(up, both, 0, 0, tiled=True, axis_index_groups=core_groups)  22.4 us
    all_to_all x1, blocking collectives, on_device(): lax.all_to_all(ends, both, 0, 0, tiled=True, axis_index_groups=core_groups)  21.6 us
    all_to_all x1, blocking collectives, on_device(): lax.all_to_all(payload, both, 0, 0, tiled=True, axis_index_groups=wave_gr...  20.7 us
    ppermute x1, starting transfers between devices, on_device(): received = lax.ppermute(send, 'kz', pairs)  9.85 us
    ppermute x1, starting transfers between devices, on_device(): swapped = lax.ppermute(forcing, 'kz', pairs)  3.24 us
    pallas_call x2, Pallas kernels, points(): pl.pallas_call(functools.partial(points_kernel, other), in_specs=[vmem] *...  2.53 us
    pallas_call x1, Pallas kernels, on_device(): pl.pallas_call(moments_kernel, in_specs=[vmem, hbm, vmem, vmem], out_spec...  2.15 us
  transfers between devices with their start and end apart: 3, of which 1 were waited for; matrix products, arithmetic and copies ran while one was open for 0% of the time, Pallas kernels for 2%

profile of v6, /device:TPU:1, one launch (start us, length us, event | category | flops | bytes accessed | tf_op | source)
XLA Modules:
  0.0 84.7 jit_solution(919586404920462120)
XLA Ops:
  0.0 3.2 %collective-permute-start = (f32[6,4,128,256]{3,2,1,0:T(8,128)}, f32[6,4,128,256]{3,2,1,0:T(8,128)S(1)}, u32[]{:S(2)}, u32[]{:S(2)}) collective-permute-start(f32[6,4,128,256]{3,2,1,0:T(8,128)} %x_ref.5), channel_id=1, source_target_pairs={{0,1},{1,0},{2,3},{3,2},{4,5},{5,4},{6,7},{7,6},{8,9},{9,8},{10,11... | collective-permute-start | bytes 9437192 | tf_op jit(solution)/shard_map/ppermute | solution.py:385
  3.2 0.7 shard_map.37
  4.0 20.7 %all_to_all.15.w_ref = f32[32,2,128]{2,1,0:T(2,128)S(1)} all-to-all(f32[32,2,128]{2,1,0:T(2,128)S(1)} %shard_map.37), channel_id=1, replica_groups={{0,1,16,17,36,37,52,53,72,73,88,89,108,109,124,125,130,131,146,147,166,..., dimensions={0} | all-to-all | bytes 65536 | tf_op jit(solution)/shard_map/all_to_all | solution.py:399
  24.7 0.7 collective-permute-start.1
  25.3 0.0 collective-permute-done.1.turn_ref
  25.3 0.0 collective-permute-done.r_ref
  25.3 2.1 %shard_map.38 = (f32[128,3,4,128]{3,2,1,0:T(4,128)S(1)}, f32[16,4,8,128]{3,2,1,0:T(8,128)S(1)}, f32[128,128]{1,0:T(8,128)S(1)}, f32[128,128]{1,0:T(8,128)S(1)}, f32[128,128]{1,0:T(8,128)S(1)}) custom-call(f32[32,2,128]{2,1,0:T(2,128)S(1)} %all_to_all.15.w_ref, f32[6,4,128,256]{3,2,1,0:T(8,128)} %x_ref.5, f32[6,4,128,256]{3,2,1,0:T(8,128)S(1)} %collective-permute-done.r_ref, ...), custom_call_target="tpu_custom_call" | custom-call | tf_op jit(solution)/shard_map/pallas_call | solution.py:402
  27.5 0.0 copy-start
  27.5 22.4 %all_to_all.16.m_ref = f32[128,3,4,128]{3,2,1,0:T(4,128)S(1)} all-to-all(f32[128,3,4,128]{3,2,1,0:T(4,128)S(1)} %get-tuple-element.12), channel_id=1, replica_groups={{0,2,4,6,8,10,12,14,16,18,20,22,24,26,28,30,32,34,36,38,40,42,44,46,48,..., dimensions={0} | all-to-all | bytes 1572864 | tf_op jit(solution)/shard_map/all_to_all | solution.py:417
  49.9 0.4 shard_map.39
  50.3 21.6 %all_to_all.17 = f32[128,8,128]{2,1,0:T(8,128)S(1)} all-to-all(f32[128,8,128]{2,1,0:T(8,128)S(1)} %shard_map.39), channel_id=1, replica_groups={{0,2,4,6,8,10,12,14,16,18,20,22,24,26,28,30,32,34,36,38,40,42,44,46,48,..., dimensions={0} | all-to-all | bytes 1048576 | tf_op jit(solution)/shard_map/all_to_all | solution.py:419
  71.9 0.2 shard_map.40
  72.0 9.8 %collective-permute-start.2 = (f32[16,8,8,128]{3,2,1,0:T(8,128)S(1)}, f32[16,8,8,128]{3,2,1,0:T(8,128)S(1)}, u32[]{:S(2)}, u32[]{:S(2)}) collective-permute-start(f32[16,8,8,128]{3,2,1,0:T(8,128)S(1)} %get-tuple-element.16), channel_id=1, source_target_pairs={{0,1},{1,0},{2,3},{3,2},{4,5},{5,4},{6,7},{7,6},{8,9},{9,8},{10,11... | collective-permute-start | bytes 1572872 | tf_op jit(solution)/shard_map/ppermute | solution.py:422
  81.9 0.0 copy-done
  81.9 1.3 %shard_map.41.refs_0_ = f32[6,4,128,256]{3,2,1,0:T(8,128)} custom-call(f32[6,4,128,256]{3,2,1,0:T(8,128)S(1)} %copy-done, f32[16,8,8,128]{3,2,1,0:T(8,128)S(1)} %get-tuple-element.18.ends, f32[128,128]{1,0:T(8,128)S(1)} %get-tuple-element.13.q_ref), custom_call_target="tpu_custom_call" | custom-call | flops 8388608 | bytes 4194304 | tf_op jit(solution)/shard_map/pallas_call | solution.py:425
  83.2 0.3 collective-permute-done.2.ends
  83.4 1.3 %shard_map.42 = f32[6,4,128,256]{3,2,1,0:T(8,128)} custom-call(f32[6,4,128,256]{3,2,1,0:T(8,128)S(1)} %copy-done, f32[16,8,8,128]{3,2,1,0:T(8,128)S(1)} %collective-permute-done.2.ends, f32[128,128]{1,0:T(8,128)S(1)} %get-tuple-element.17.q_ref, f32[6,4,128,256]{3,2,1,0:T(8,128)} %shard_map.41.refs_0_), custom_call_target="tpu_custom_call", output_to_operand_aliasing={{}: (3, {})} | custom-call | flops 8388608 | bytes 4194304 | tf_op jit(solution)/shard_map/pallas_call | solution.py:425
Async XLA Ops:
  0.0 25.3 %collective-permute-start = (f32[6,4,128,256]{3,2,1,0:T(8,128)}, f32[6,4,128,256]{3,2,1,0:T(8,128)S(1)}, u32[]{:S(2)}, u32[]{:S(2)}) collective-permute-start(f32[6,4,128,256]{3,2,1,0:T(8,128)} %x_ref.5), channel_id=1, source_target_pairs={{0,1},{1,0},{2,3},{3,2},{4,5},{5,4},{6,7},{7,6},{8,9},{9,8},{10,11... | collective-permute-start | bytes 9437192 | tf_op jit(solution)/shard_map/ppermute | solution.py:385
  24.7 0.7 collective-permute-start.1
  27.5 54.4 %copy-start = (f32[6,4,128,256]{3,2,1,0:T(8,128)S(1)}, f32[6,4,128,256]{3,2,1,0:T(8,128)}, u32[]{:S(2)}) copy-start(f32[6,4,128,256]{3,2,1,0:T(8,128)} %x_ref.5) | copy-start | bytes 9437188
  72.0 11.4 %collective-permute-start.2 = (f32[16,8,8,128]{3,2,1,0:T(8,128)S(1)}, f32[16,8,8,128]{3,2,1,0:T(8,128)S(1)}, u32[]{:S(2)}, u32[]{:S(2)}) collective-permute-start(f32[16,8,8,128]{3,2,1,0:T(8,128)S(1)} %get-tuple-element.16), channel_id=1, source_target_pairs={{0,1},{1,0},{2,3},{3,2},{4,5},{5,4},{6,7},{7,6},{8,9},{9,8},{10,11... | collective-permute-start | bytes 1572872 | tf_op jit(solution)/shard_map/ppermute | solution.py:422

commit v7 on v6

--- a/solution.py
+++ b/solution.py
@@ -296,9 +296,10 @@
         @pl.loop(0, GRP, unroll=2)
         def _(i):
             ratio = ratio_ref[pl.ds(pl.multiple_of(8 * i, 8), 8), :]
+            numbers = jnp.swapaxes(b_ref[pl.ds(pl.multiple_of(8 * i, 8), 8)], 0, 1)
             for c in range(4):
-                a = b_ref[pl.ds(64 * i + c, 8, stride=8), :]
-                b = b_ref[pl.ds(64 * i + 4 + c, 8, stride=8), :]
+                a = numbers[c]
+                b = numbers[4 + c]
                 x = ratio * (a + b) + mid_ref[i, c]
                 lower[i, c] = a
                 lower[i, 4 + c] = x
@@ -409,7 +410,7 @@
         ],
         scratch_shapes=[
             pltpu.VMEM(half_shape, F32),
-            pltpu.VMEM((NUM * CHIPS, 128), F32),
+            pltpu.VMEM((NUM * (CHIPS + 8), 128), F32),
             pltpu.SemaphoreType.DMA((4,)),
         ],
         compiler_params=params,
@@ -417,7 +418,6 @@
     blocks = lax.all_to_all(up, both, 0, 0, tiled=True, axis_index_groups=core_groups)
     (ends,) = local_call(solve_kernel, (blocks, q_own), ((CHIPS, 8, 128),))
     ends = lax.all_to_all(ends, both, 0, 0, tiled=True, axis_index_groups=core_groups)
-    ends = ends.reshape(8 * CHIPS, 128)
     own, send = local_call(middle_kernel, (ends, mid, ratio), ((GRP, 8, 8, 128),) * 2)
     received = lax.ppermute(send, "kz", pairs)
 

time: 84.9 us -> 84.9 us (level)
  no operation moved by 1% of the time
where the time goes in v7:
time: 84.9 us; the launch traced here: 84.7 us
  blocking collectives  64.7 us (76%)
  starting transfers between devices  13.7 us (16%)
  Pallas kernels  5.94 us (7%)
    all_to_all x1, blocking collectives, on_device(): lax.all_to_all(up, both, 0, 0, tiled=True, axis_index_groups=core_groups)  22.4 us
    all_to_all x1, blocking collectives, on_device(): lax.all_to_all(ends, both, 0, 0, tiled=True, axis_index_groups=core_groups)  21.6 us
    all_to_all x1, blocking collectives, on_device(): lax.all_to_all(payload, both, 0, 0, tiled=True, axis_index_groups=wave_gr...  20.7 us
    ppermute x1, starting transfers between devices, on_device(): received = lax.ppermute(send, 'kz', pairs)  9.85 us
    ppermute x1, starting transfers between devices, on_device(): swapped = lax.ppermute(forcing, 'kz', pairs)  3.24 us
    pallas_call x2, Pallas kernels, points(): pl.pallas_call(functools.partial(points_kernel, other), in_specs=[vmem] *...  2.53 us
    pallas_call x1, Pallas kernels, on_device(): pl.pallas_call(moments_kernel, in_specs=[vmem, hbm, vmem, vmem], out_spec...  2.15 us
  transfers between devices with their start and end apart: 3, of which 1 were waited for; matrix products, arithmetic and copies ran while one was open for 0% of the time, Pallas kernels for 2%

profile of v7, /device:TPU:1, one launch (start us, length us, event | category | flops | bytes accessed | tf_op | source)
XLA Modules:
  0.0 84.7 jit_solution(14251648559233422318)
XLA Ops:
  0.0 3.2 %collective-permute-start = (f32[6,4,128,256]{3,2,1,0:T(8,128)}, f32[6,4,128,256]{3,2,1,0:T(8,128)S(1)}, u32[]{:S(2)}, u32[]{:S(2)}) collective-permute-start(f32[6,4,128,256]{3,2,1,0:T(8,128)} %x_ref.5), channel_id=1, source_target_pairs={{0,1},{1,0},{2,3},{3,2},{4,5},{5,4},{6,7},{7,6},{8,9},{9,8},{10,11... | collective-permute-start | bytes 9437192 | tf_op jit(solution)/shard_map/ppermute | solution.py:386
  3.2 0.7 shard_map.37
  4.0 20.7 %all_to_all.15.w_ref = f32[32,2,128]{2,1,0:T(2,128)S(1)} all-to-all(f32[32,2,128]{2,1,0:T(2,128)S(1)} %shard_map.37), channel_id=1, replica_groups={{0,1,16,17,36,37,52,53,72,73,88,89,108,109,124,125,130,131,146,147,166,..., dimensions={0} | all-to-all | bytes 65536 | tf_op jit(solution)/shard_map/all_to_all | solution.py:400
  24.7 0.7 collective-permute-start.1
  25.3 0.0 collective-permute-done.1.turn_ref
  25.3 0.0 collective-permute-done.r_ref
  25.3 2.1 %shard_map.38 = (f32[128,3,4,128]{3,2,1,0:T(4,128)S(1)}, f32[16,4,8,128]{3,2,1,0:T(8,128)S(1)}, f32[128,128]{1,0:T(8,128)S(1)}, f32[128,128]{1,0:T(8,128)S(1)}, f32[128,128]{1,0:T(8,128)S(1)}) custom-call(f32[32,2,128]{2,1,0:T(2,128)S(1)} %all_to_all.15.w_ref, f32[6,4,128,256]{3,2,1,0:T(8,128)} %x_ref.5, f32[6,4,128,256]{3,2,1,0:T(8,128)S(1)} %collective-permute-done.r_ref, ...), custom_call_target="tpu_custom_call" | custom-call | tf_op jit(solution)/shard_map/pallas_call | solution.py:403
  27.5 0.0 copy-start
  27.5 22.4 %all_to_all.16.m_ref = f32[128,3,4,128]{3,2,1,0:T(4,128)S(1)} all-to-all(f32[128,3,4,128]{3,2,1,0:T(4,128)S(1)} %get-tuple-element.12), channel_id=1, replica_groups={{0,2,4,6,8,10,12,14,16,18,20,22,24,26,28,30,32,34,36,38,40,42,44,46,48,..., dimensions={0} | all-to-all | bytes 1572864 | tf_op jit(solution)/shard_map/all_to_all | solution.py:418
  49.9 0.4 shard_map.39
  50.3 21.6 %all_to_all.17.b_ref = f32[128,8,128]{2,1,0:T(8,128)S(1)} all-to-all(f32[128,8,128]{2,1,0:T(8,128)S(1)} %shard_map.39), channel_id=1, replica_groups={{0,2,4,6,8,10,12,14,16,18,20,22,24,26,28,30,32,34,36,38,40,42,44,46,48,..., dimensions={0} | all-to-all | bytes 1048576 | tf_op jit(solution)/shard_map/all_to_all | solution.py:420
  71.9 0.2 shard_map.40
  72.0 9.8 %collective-permute-start.2 = (f32[16,8,8,128]{3,2,1,0:T(8,128)S(1)}, f32[16,8,8,128]{3,2,1,0:T(8,128)S(1)}, u32[]{:S(2)}, u32[]{:S(2)}) collective-permute-start(f32[16,8,8,128]{3,2,1,0:T(8,128)S(1)} %get-tuple-element.16), channel_id=1, source_target_pairs={{0,1},{1,0},{2,3},{3,2},{4,5},{5,4},{6,7},{7,6},{8,9},{9,8},{10,11... | collective-permute-start | bytes 1572872 | tf_op jit(solution)/shard_map/ppermute | solution.py:422
  81.9 0.0 copy-done
  81.9 1.3 %shard_map.41.refs_0_ = f32[6,4,128,256]{3,2,1,0:T(8,128)} custom-call(f32[6,4,128,256]{3,2,1,0:T(8,128)S(1)} %copy-done, f32[16,8,8,128]{3,2,1,0:T(8,128)S(1)} %get-tuple-element.18.ends, f32[128,128]{1,0:T(8,128)S(1)} %get-tuple-element.13.q_ref), custom_call_target="tpu_custom_call" | custom-call | flops 8388608 | bytes 4194304 | tf_op jit(solution)/shard_map/pallas_call | solution.py:425
  83.2 0.3 collective-permute-done.2.ends
  83.4 1.3 %shard_map.42 = f32[6,4,128,256]{3,2,1,0:T(8,128)} custom-call(f32[6,4,128,256]{3,2,1,0:T(8,128)S(1)} %copy-done, f32[16,8,8,128]{3,2,1,0:T(8,128)S(1)} %collective-permute-done.2.ends, f32[128,128]{1,0:T(8,128)S(1)} %get-tuple-element.17.q_ref, f32[6,4,128,256]{3,2,1,0:T(8,128)} %shard_map.41.refs_0_), custom_call_target="tpu_custom_call", output_to_operand_aliasing={{}: (3, {})} | custom-call | flops 8388608 | bytes 4194304 | tf_op jit(solution)/shard_map/pallas_call | solution.py:425
Async XLA Ops:
  0.0 25.3 %collective-permute-start = (f32[6,4,128,256]{3,2,1,0:T(8,128)}, f32[6,4,128,256]{3,2,1,0:T(8,128)S(1)}, u32[]{:S(2)}, u32[]{:S(2)}) collective-permute-start(f32[6,4,128,256]{3,2,1,0:T(8,128)} %x_ref.5), channel_id=1, source_target_pairs={{0,1},{1,0},{2,3},{3,2},{4,5},{5,4},{6,7},{7,6},{8,9},{9,8},{10,11... | collective-permute-start | bytes 9437192 | tf_op jit(solution)/shard_map/ppermute | solution.py:386
  24.7 0.7 collective-permute-start.1
  27.5 54.4 %copy-start = (f32[6,4,128,256]{3,2,1,0:T(8,128)S(1)}, f32[6,4,128,256]{3,2,1,0:T(8,128)}, u32[]{:S(2)}) copy-start(f32[6,4,128,256]{3,2,1,0:T(8,128)} %x_ref.5) | copy-start | bytes 9437188
  72.0 11.4 %collective-permute-start.2 = (f32[16,8,8,128]{3,2,1,0:T(8,128)S(1)}, f32[16,8,8,128]{3,2,1,0:T(8,128)S(1)}, u32[]{:S(2)}, u32[]{:S(2)}) collective-permute-start(f32[16,8,8,128]{3,2,1,0:T(8,128)S(1)} %get-tuple-element.16), channel_id=1, source_target_pairs={{0,1},{1,0},{2,3},{3,2},{4,5},{5,4},{6,7},{7,6},{8,9},{9,8},{10,11... | collective-permute-start | bytes 1572872 | tf_op jit(solution)/shard_map/ppermute | solution.py:422
